TPU v7x, 128 devices: a whole 4x4x4 slice. The times are simulated.
128 devices in a mesh: gx: 16 (over y, z), gy: 4 (over x_hi, core), gz: 2 (over x_lo).
Axes of the slice: x: 4 (x_hi: 2, x_lo: 2; x = x_hi * 2 + x_lo), y: 4, z: 4, core: 2. Of those that a mesh axis runs over, the one named last changes fastest.
Arguments:
- blocks: bfloat16 [4, 16, 128, 256, 256], P('gy', 'gx'), may hold values from -0.0625 to 0.0625
- block_rows: int32 [4, 16, 128], P('gy', 'gx'), may hold values from 0 to 63
- block_cols: int32 [4, 16, 128], P('gy', 'gx'), may hold values from 0 to 15
- probe_bits: int32 [65536, 256], P(('gy', 'gx'), 'gz'), may hold values from 0 to 1
- shift: float32 [65536], P(('gy', 'gx')), may hold values from 0 to 0.7
Outputs:
- forms: float32 [3, 256], P(None, 'gz')
- last_term: float32 [65536, 256], P(('gy', 'gx'), 'gz')
All inputs are finite; a program needn't handle non-finite values.
Results may differ from a plain program's by a relative error of at most 0.02.
Values may be sent and summed in bfloat16 or wider, within the bound.
A program may use at most 128 MiB of HBM per device.

v0:
```python
import jax
import jax.numpy as jnp
from jax import lax
from jax.sharding import PartitionSpec as P


def copy_for_each(array, axis):
    copies = jnp.broadcast_to(array, (lax.axis_size(axis), *array.shape))
    return lax.all_to_all(copies, axis, split_axis=0, concat_axis=0, tiled=True)


def joined_along(pieces, dim):
    lengths = list(pieces.shape[1:])
    lengths[dim] *= pieces.shape[0]
    return jnp.moveaxis(pieces, 0, dim).reshape(lengths)


def collect(array, axis, dim):
    pieces = copy_for_each(array, axis)
    return joined_along(pieces, dim)


def in_blocks(array, dim, count):
    before, after = (array.shape[:dim], array.shape[dim + 1 :])
    return jnp.moveaxis(array.reshape(*before, count, -1, *after), dim, 0)


def sum_at_owner(array, axis, dim):
    count = lax.axis_size(axis)
    pieces = lax.all_to_all(in_blocks(array, dim, count), axis, 0, 0, tiled=True)
    return jnp.sum(pieces.astype(jnp.float32), axis=0)


def taken_together(array, axis):
    return copy_for_each(array, axis).sum(axis=0)


def body(blocks, block_rows, block_cols, probe_bits, shift):
    tile_blocks = blocks[0, 0]
    rows_here = block_rows[0, 0]
    cols_here = block_cols[0, 0]
    block_size = tile_blocks.shape[1]
    local_rows = shift.shape[0]
    probe_count = probe_bits.shape[1]
    tile_rows = local_rows // block_size * lax.axis_size("gx")
    signs = (2 * probe_bits - 1).astype(jnp.float32)

    def apply_operator(field):
        rounded = field.astype(jnp.bfloat16)
        whole = collect(rounded, "gy", 0)
        whole = whole.reshape(whole.shape[0] // block_size, block_size, probe_count)
        picked = whole[cols_here]
        product = jnp.einsum(
            "kab,kbp->kap", tile_blocks, picked, preferred_element_type=jnp.float32
        )
        partial_rows = (
            jnp.zeros((tile_rows, block_size, probe_count), jnp.float32).at[rows_here].add(product)
        )
        partial_rows = partial_rows.reshape(tile_rows * block_size, probe_count)
        summed = sum_at_owner(partial_rows.astype(jnp.bfloat16), "gx", 0)
        return summed + shift[:, None] * field

    first = apply_operator(signs)
    second = 2.0 * apply_operator(first) - signs
    third = 2.0 * apply_operator(second) - first
    local_forms = jnp.stack(
        [
            jnp.sum(signs * first, axis=0),
            jnp.sum(signs * second, axis=0),
            jnp.sum(signs * third, axis=0),
        ]
    )
    forms = taken_together(local_forms, ("gx", "gy"))
    return (forms, third)


def solution(mesh):
    return jax.shard_map(
        body,
        mesh=mesh,
        in_specs=(
            P("gy", "gx", None, None, None),
            P("gy", "gx", None),
            P("gy", "gx", None),
            P(("gy", "gx"), "gz"),
            P(("gy", "gx")),
        ),
        out_specs=(P(None, "gz"), P(("gy", "gx"), "gz")),
        check_vma=False,
    )
```

profile of v0, /device:TPU:0, one launch (start us, length us, event | category | flops | bytes accessed | tf_op | source)
XLA Modules:
  0.0 509.3 jit_solution(15199909525136784446)
XLA Ops:
  0.6 1.1 convert_convert_fusion
  1.8 1.1 broadcast_in_dim.8
  2.9 4.4 all-to-all-start
  7.3 0.7 fusion.16
  7.9 0.7 fusion.15
  8.6 14.6 %all-to-all-done = bf16[4,1024,128]{2,1,0:T(8,128)(2,1)S(1)} async-done(((bf16[4,1024,128]{2,1,0:T(8,128)(2,1)}), bf16[4,1024,128]{2,1,0:T(8,128)(2,1)S(1)}, u32[]{:S(2)}, u32[]{:S(2)}) %all-to-all-start) | async-done | bytes 1048608 | tf_op jit(solution)/shard_map/all_to_all | solution.py:9
  23.2 6.6 %gather_fusion = bf16[128,256,128]{2,1,0:T(8,128)(2,1)} fusion(bf16[16,256,128]{2,1,0:T(8,128)(2,1)S(1)} %bitcast.39, s32[1024]{0:T(1024)S(1)} %pad_clamp_fusion), kind=kCustom, calls=%fused_computation | custom fusion | bytes 16777728 | tf_op jit(solution)/shard_map/gather | solution.py:52
  29.8 17.2 %fusion.6 = f32[128,256,128]{1,2,0:T(8,128)} fusion(bf16[128,256,128]{2,1,0:T(8,128)(2,1)} %gather_fusion, bf16[1,1,128,256,256]{4,3,2,1,0:T(8,128)(2,1)} %param.5), kind=kOutput, calls=%fused_computation.12 | convolution fusion | flops 2147483648 | bytes 41943040 | tf_op jit(solution)/shard_map/kab,kbp->kap/dot_general | solution.py:53
  47.0 17.4 %copy.23 = f32[128,256,128]{2,1,0:T(8,128)} copy(f32[128,256,128]{1,2,0:T(8,128)} %fusion.6) | data formatting | bytes 33554432 | tf_op jit(solution)/shard_map/kab,kbp->kap/dot_general | solution.py:53
  64.4 4.2 broadcast.48.clone
  68.6 38.2 %scatter_fusion = f32[64,256,128]{2,1,0:T(8,128)} fusion(f32[64,256,128]{2,1,0:T(8,128)} %broadcast.48.clone, s32[128]{0:T(128)S(1)} %fusion.15, f32[128,256,128]{2,1,0:T(8,128)} %copy.23), kind=kCustom, calls=%fused_computation.3 | custom fusion | flops 4194304 | bytes 50332160 | tf_op jit(solution)/shard_map/scatter-add | solution.py:57
  106.8 4.1 convert_element_type.44
  110.9 0.0 copy-start
  110.9 0.0 copy-start.1
  110.9 58.8 %all_to_all.35 = bf16[16,1024,128]{2,1,0:T(8,128)(2,1)S(1)} all-to-all(bf16[16,1024,128]{2,1,0:T(8,128)(2,1)S(1)} %bitcast.42), channel_id=1, replica_groups=mesh['gx'=16,'gy'=4,'gz'=2] {'gx'}, dimensions={0} | all-to-all | bytes 8388608 | tf_op jit(solution)/shard_map/all_to_all | solution.py:30
  169.8 0.6 convert_reduce_fusion.2
  170.3 0.0 copy-done
  170.3 0.0 copy-done.1
  170.4 0.2 fusion.17
  170.6 0.1 broadcast_in_dim.9
  170.7 18.4 %all_to_all.36 = bf16[4,1024,128]{2,1,0:T(8,128)(2,1)S(1)} all-to-all(bf16[4,1024,128]{2,1,0:T(8,128)(2,1)S(1)} %broadcast_in_dim.9), channel_id=1, replica_groups=mesh['gx'=16,'gy'=4,'gz'=2] {'gy'}, dimensions={0} | all-to-all | bytes 2097152 | tf_op jit(solution)/shard_map/all_to_all | solution.py:9
  189.1 6.6 %gather_fusion.1 = bf16[128,256,128]{2,1,0:T(8,128)(2,1)} fusion(bf16[16,256,128]{2,1,0:T(8,128)(2,1)S(1)} %bitcast.41, s32[1024]{0:T(1024)S(1)} %pad_clamp_fusion), kind=kCustom, calls=%fused_computation.1 | custom fusion | bytes 16777728 | tf_op jit(solution)/shard_map/gather | solution.py:52
  195.7 17.2 %fusion.9 = f32[128,256,128]{1,2,0:T(8,128)} fusion(bf16[128,256,128]{2,1,0:T(8,128)(2,1)} %gather_fusion.1, bf16[1,1,128,256,256]{4,3,2,1,0:T(8,128)(2,1)} %param.5), kind=kOutput, calls=%fused_computation.13 | convolution fusion | flops 2147483648 | bytes 41943040 | tf_op jit(solution)/shard_map/kab,kbp->kap/dot_general | solution.py:53
  212.8 17.4 %copy.25 = f32[128,256,128]{2,1,0:T(8,128)} copy(f32[128,256,128]{1,2,0:T(8,128)} %fusion.9) | data formatting | bytes 33554432 | tf_op jit(solution)/shard_map/kab,kbp->kap/dot_general | solution.py:53
  230.2 4.2 broadcast.48.clone.1
  234.5 38.2 %scatter_fusion.1 = f32[64,256,128]{2,1,0:T(8,128)} fusion(f32[64,256,128]{2,1,0:T(8,128)} %broadcast.48.clone.1, s32[128]{0:T(128)S(1)} %fusion.15, f32[128,256,128]{2,1,0:T(8,128)} %copy.25), kind=kCustom, calls=%fused_computation.4 | custom fusion | flops 4194304 | bytes 50332160 | tf_op jit(solution)/shard_map/scatter-add | solution.py:57
  272.6 4.1 convert_element_type.48
  276.8 54.7 %all_to_all.37 = bf16[16,1024,128]{2,1,0:T(8,128)(2,1)S(1)} all-to-all(bf16[16,1024,128]{2,1,0:T(8,128)(2,1)S(1)} %bitcast.43), channel_id=1, replica_groups=mesh['gx'=16,'gy'=4,'gz'=2] {'gx'}, dimensions={0} | all-to-all | bytes 8388608 | tf_op jit(solution)/shard_map/all_to_all | solution.py:30
  331.4 0.6 convert_reduce_fusion.1
  332.0 0.2 fusion.18
  332.3 0.1 broadcast_in_dim.10
  332.4 18.4 %all_to_all.38 = bf16[4,1024,128]{2,1,0:T(8,128)(2,1)S(1)} all-to-all(bf16[4,1024,128]{2,1,0:T(8,128)(2,1)S(1)} %broadcast_in_dim.10), channel_id=1, replica_groups=mesh['gx'=16,'gy'=4,'gz'=2] {'gy'}, dimensions={0} | all-to-all | bytes 2097152 | tf_op jit(solution)/shard_map/all_to_all | solution.py:9
  350.8 6.6 %gather_fusion.2 = bf16[128,256,128]{2,1,0:T(8,128)(2,1)} fusion(bf16[16,256,128]{2,1,0:T(8,128)(2,1)S(1)} %bitcast.40, s32[1024]{0:T(1024)S(1)} %pad_clamp_fusion), kind=kCustom, calls=%fused_computation.2 | custom fusion | bytes 16777728 | tf_op jit(solution)/shard_map/gather | solution.py:52
  357.4 17.2 %fusion.12 = f32[128,256,128]{1,2,0:T(8,128)} fusion(bf16[128,256,128]{2,1,0:T(8,128)(2,1)} %gather_fusion.2, bf16[1,1,128,256,256]{4,3,2,1,0:T(8,128)(2,1)} %param.5), kind=kOutput, calls=%fused_computation.14 | convolution fusion | flops 2147483648 | bytes 41943040 | tf_op jit(solution)/shard_map/kab,kbp->kap/dot_general | solution.py:53
  374.5 17.4 %copy.27 = f32[128,256,128]{2,1,0:T(8,128)} copy(f32[128,256,128]{1,2,0:T(8,128)} %fusion.12) | data formatting | bytes 33554432 | tf_op jit(solution)/shard_map/kab,kbp->kap/dot_general | solution.py:53
  391.9 4.2 broadcast.48
  396.2 38.2 %scatter_fusion.2 = f32[64,256,128]{2,1,0:T(8,128)} fusion(f32[64,256,128]{2,1,0:T(8,128)} %broadcast.48, s32[128]{0:T(128)S(1)} %fusion.15, f32[128,256,128]{2,1,0:T(8,128)} %copy.27), kind=kCustom, calls=%fused_computation.5 | custom fusion | flops 4194304 | bytes 50332160 | tf_op jit(solution)/shard_map/scatter-add | solution.py:57
  434.3 4.1 convert_element_type.52
  438.5 54.1 %all_to_all.39 = bf16[16,1024,128]{2,1,0:T(8,128)(2,1)S(1)} all-to-all(bf16[16,1024,128]{2,1,0:T(8,128)(2,1)S(1)} %bitcast.44), channel_id=1, replica_groups=mesh['gx'=16,'gy'=4,'gz'=2] {'gx'}, dimensions={0} | all-to-all | bytes 8388608 | tf_op jit(solution)/shard_map/all_to_all | solution.py:30
  492.6 0.6 convert_reduce_fusion
  493.2 1.2 multiply_reduce_fusion.2
  494.4 14.3 %all_to_all.40 = f32[64,3,128]{2,1,0:T(4,128)S(1)} all-to-all(f32[64,3,128]{2,1,0:T(4,128)S(1)} %broadcast_in_dim.11), channel_id=1, replica_groups=mesh['gx'=16,'gy'=4,'gz'=2] {'gx','gy'}, dimensions={0} | all-to-all | bytes 196608 | tf_op jit(solution)/shard_map/all_to_all | solution.py:9
  508.7 0.7 reduce_sum.69
  (3 shorter events, 0.0 us)
Async XLA Ops:
  2.9 20.3 %all-to-all-start = ((bf16[4,1024,128]{2,1,0:T(8,128)(2,1)}), bf16[4,1024,128]{2,1,0:T(8,128)(2,1)S(1)}, u32[]{:S(2)}, u32[]{:S(2)}) async-start(bf16[4,1024,128]{2,1,0:T(8,128)(2,1)} %broadcast_in_dim.8), calls=%async_computation | async-start | bytes 2097152 | tf_op jit(solution)/shard_map/all_to_all | solution.py:9
  110.9 59.5 %copy-start = (s32[1024,128]{1,0:T(8,128)S(1)}, s32[1024,128]{1,0:T(8,128)}, u32[]{:S(2)}) copy-start(s32[1024,128]{1,0:T(8,128)} %param.8) | copy-start | bytes 1572868
  110.9 59.5 %copy-start.1 = (f32[1024]{0:T(1024)S(1)}, f32[1024]{0:T(1024)}, u32[]{:S(2)}) copy-start(f32[1024]{0:T(1024)} %param.9) | copy-start | bytes 12292
where the time goes:
time: 512 us; the launch traced here: 509 us
  blocking collectives  219 us (43%)
  other arithmetic  133 us (26%)
  local copies, waits for them, and re-layouts  86.1 us (17%)
  matrix products  51.5 us (10%)
  waiting for transfers between devices  14.6 us (3%)
    all_to_all x3, blocking collectives, sum_at_owner(): lax.all_to_all(in_blocks(array, dim, count), axis, 0, 0, tiled=True)  168 us
    scatter-add x3, other arithmetic, apply_operator(): jnp.zeros((tile_rows, block_size, probe_count), jnp.float32).at[rows_here]  114 us
    dot_general x3, local copies, waits for them, and re-layouts, apply_operator(): jnp.einsum('kab,kbp->kap', tile_blocks, picked, preferred_element_type=jn...  52.2 us
    dot_general x3, matrix products, apply_operator(): jnp.einsum('kab,kbp->kap', tile_blocks, picked, preferred_element_type=jn...  51.5 us
    all_to_all x3, blocking collectives, copy_for_each(): return lax.all_to_all(copies, axis, split_axis=0, concat_axis=0, tiled=True)  51.1 us
    gather x3, local copies, waits for them, and re-layouts, apply_operator(): picked = whole[cols_here]  19.7 us
    all_to_all x1, waiting for transfers between devices, copy_for_each(): return lax.all_to_all(copies, axis, split_axis=0, concat_axis=0, tiled=True)  14.6 us
    another operation x3, local copies, waits for them, and re-layouts  12.7 us
  transfers between devices with their start and end apart: 1, of which 1 were waited for; matrix products, arithmetic and copies ran while one was open for 0% of the time, Pallas kernels for 0%

commit v1 on v0

v1 whole, which is shorter than its diff:
```python
import jax
import jax.numpy as jnp
from jax import lax
from jax.experimental import pallas as pl
from jax.experimental.pallas import tpu as pltpu
from jax.sharding import PartitionSpec as P

BS = 256
KT = 128
TR = 64
TC = 16
NP = 128
PC = 4
HB = BS // 2
QB = BS // 4
LOC = PC * BS
F32 = jnp.float32
BF16 = jnp.bfloat16
UNROLL = 4

CHUNKS = ((2, 0), (2, 1), (1, 2), (1, 3), (1, 0), (1, 1),
          (2, 2), (2, 3), (3, 0), (3, 1), (3, 2), (3, 3))
FIRST = ((0, 4), (6, 4), (4, 2), (10, 2))
SECOND = ((0, 2), (3, 2), (2, 1), (5, 1))


def kernel(code, last, blocks_hbm, bits, shift_in, out_hbm, forms,
           blocks, s, w, land, t, z, shift, p, r1, q, qown, r2, fsum, fs, fr,
           load_sem, out_sem, psend, qsend, rs_recv, sib_send, part_send, fwd_send,
           sib_recv, fwd_recv, part_recv, fsend, frecv):
    gx, gy, gz = lax.axis_index("gx"), lax.axis_index("gy"), lax.axis_index("gz")
    y, zc = gx // 4, gx % 4
    sib = {"gx": gx, "gy": gy + 1 - 2 * (gy % 2), "gz": gz}
    partner_gy = (gy + 2) % 4
    part = {"gx": gx, "gy": partner_gy, "gz": gz}

    def at_y(d):
        return {"gx": (y + d) % 4 * 4 + zc, "gy": gy, "gz": gz}

    def at_z(d):
        return {"gx": y * 4 + (zc + d) % 4, "gy": gy, "gz": gz}

    def at_gy(d):
        return {"gx": gx, "gy": (gy + d) % 4, "gz": gz}

    load = pltpu.make_async_copy(blocks_hbm, blocks, load_sem)
    load.start()

    barrier = pltpu.get_barrier_semaphore()
    for d in (1, 2, 3):
        for there in (at_y, at_z, at_gy):
            pl.semaphore_signal(barrier, inc=1, device_id=there(d), device_id_type=pl.DeviceIdType.MESH)

    def remote(src, dst, send, recv, where):
        return pltpu.make_async_remote_copy(
            src_ref=src, dst_ref=dst, send_sem=send, recv_sem=recv,
            device_id=where, device_id_type=pl.DeviceIdType.MESH)

    def wait_for(ref, sem):
        pltpu.make_async_copy(ref, ref, sem).wait()

    signs = (2 * bits[...] - 1).astype(F32)
    z[...] = signs
    t[0] = signs
    t[1] = jnp.zeros((LOC, NP), F32)
    for b in range(PC):
        land[0, gy * PC + b] = signs[b * BS:(b + 1) * BS].astype(BF16)
    for c in range(LOC // NP):
        shift[c * NP:(c + 1) * NP] = jnp.broadcast_to(shift_in[c:c + 1], (NP, NP)).T
    fsum[...] = jnp.zeros_like(fsum)
    s[KT] = jnp.zeros((BS, NP), BF16)

    def share(par, b):
        mine = land.at[par, gy * PC + b]
        remote(mine, mine, part_send.at[par], part_recv.at[par, b], part).start()
        remote(mine, mine, sib_send.at[par], sib_recv.at[par], sib).start()

    def forward(par, b):
        got = land.at[par, partner_gy * PC + b]
        wait_for(got, part_recv.at[par, b])
        remote(got, got, fwd_send.at[par], fwd_recv.at[par], sib).start()

    pl.semaphore_wait(barrier, 9)
    for b in range(PC):
        share(0, b)
    for b in range(PC):
        forward(0, b)
    load.wait()

    def apply(a, _):
        par = lax.rem(a, 2)
        nxt = 1 - par
        four = land.at[par, pl.ds(0, PC)]
        for sem in (sib_recv, fwd_recv):
            wait_for(four, sem.at[par])
        for sem in (sib_send, part_send, fwd_send):
            wait_for(four, sem.at[par])
        w[...] = land[par]

        def block(k, carry):
            acc, prev = carry
            e = code[k]
            row = e // (KT * TC)
            keep = (row == prev).astype(F32)
            prod = jnp.dot(blocks[e % KT], w[e // KT % TC], preferred_element_type=F32)
            acc = acc * keep + prod
            s[k] = acc.astype(BF16)
            return acc, row

        def group(g, carry):
            for u in range(UNROLL):
                carry = block(g * UNROLL + u, carry)
            return carry

        lax.fori_loop(0, KT // UNROLL, group, (jnp.zeros((BS, NP), F32), jnp.int32(-1)))

        first_axis, second_axis = (at_y, at_z), (at_z, at_y)

        def row_of(h, b, d1, d2):
            dy, dz = (d1, d2) if h == 0 else (d2, d1)
            return last[((y + dy) % 4 * 4 + (zc + dz) % 4) * PC + b]

        def half(h):
            return slice(h * HB, (h + 1) * HB)

        def send(buf, land_in, h, b, table, m, sem, axis, stage):
            at, n = table[m]
            src = buf.at[h, b, pl.ds(at, n)]
            remote(src, land_in.at[par, h, b, pl.ds(at, n)], sem,
                   rs_recv.at[par, h, b, stage, m], axis(1 if m % 2 == 0 else 3)).start()

        def arrived(land_in, h, b, table, m, stage):
            at, n = table[m]
            wait_for(land_in.at[par, h, b, pl.ds(at, n)], rs_recv.at[par, h, b, stage, m])

        def step1(b):
            for h in (0, 1):
                for m in (0, 1, 2, 3):
                    at, n = FIRST[m]
                    for c in range(at, at + n):
                        p[h, b, c] = s[row_of(h, b, *CHUNKS[c]), half(h)]
                    if m < 2:
                        send(p, r1, h, b, FIRST, m, psend, first_axis[h], 0)

        def step2(b):
            for m in (0, 1):
                for h in (0, 1):
                    arrived(r1, h, b, FIRST, m, 0)
                    at, n = FIRST[m + 2]
                    came = FIRST[m][0]
                    for c in range(n):
                        p[h, b, at + c] = (p[h, b, at + c].astype(F32) + r1[par, h, b, came + c].astype(F32)).astype(BF16)
                    send(p, r1, h, b, FIRST, m + 2, psend, first_axis[h], 0)

        def step3(b):
            for h in (0, 1):
                for m in (2, 3):
                    arrived(r1, h, b, FIRST, m, 0)
                sums = {}
                for d in (2, 1, 3, 0):
                    up, down = (4 + d, 8 + d) if d < 2 else (d, 8 + d)
                    sums[d] = (s[row_of(h, b, 0, d), half(h)].astype(F32)
                               + r1[par, h, b, up].astype(F32) + r1[par, h, b, down].astype(F32))
                    if d == 2:
                        q[h, b, 0] = sums[2][:QB].astype(BF16)
                        q[h, b, 3] = sums[2][QB:].astype(BF16)
                    if d == 1:
                        q[h, b, 2] = sums[1][:QB].astype(BF16)
                        q[h, b, 1] = sums[1][QB:].astype(BF16)
                        send(q, r2, h, b, SECOND, 0, qsend, second_axis[h], 1)
                    if d == 3:
                        q[h, b, 4] = sums[3][:QB].astype(BF16)
                        q[h, b, 5] = sums[3][QB:].astype(BF16)
                        send(q, r2, h, b, SECOND, 1, qsend, second_axis[h], 1)
                    if d == 0:
                        qown[h, b] = sums[0]

        def step4(b):
            for m in (0, 1):
                for h in (0, 1):
                    arrived(r2, h, b, SECOND, m, 1)
                    at, came = SECOND[m + 2][0], SECOND[m][0]
                    q[h, b, at] = (q[h, b, at].astype(F32) + r2[par, h, b, came].astype(F32)).astype(BF16)
                    send(q, r2, h, b, SECOND, m + 2, qsend, second_axis[h], 1)

        factor = jnp.where(a == 0, 1.0, 2.0).astype(F32)

        def step5(b):
            for h in (0, 1):
                for m in (2, 3):
                    arrived(r2, h, b, SECOND, m, 1)
                for o, (x1, x2) in ((0, (2, 4)), (QB, (1, 5))):
                    m_w = qown[h, b, o:o + QB] + r2[par, h, b, x1].astype(F32) + r2[par, h, b, x2].astype(F32)
                    at = b * BS + h * HB + o
                    rows = slice(at, at + QB)
                    new = factor * (m_w + shift[rows] * t[par, rows]) - t[nxt, rows]
                    t[nxt, rows] = new
                    land[nxt, gy * PC + b, h * HB + o:h * HB + o + QB] = new.astype(BF16)
                    fsum[a] += jnp.sum((z[rows] * new).reshape(QB // 8, 8, NP), axis=0)

            @pl.when(a < 2)
            def _():
                share(nxt, b)

        def step6(b):
            @pl.when(a < 2)
            def _():
                forward(nxt, b)

        step1(0)
        for now in range(1, PC + 5):
            for lag, step in ((0, step1), (1, step2), (2, step3), (3, step4), (4, step5), (5, step6)):
                b = now - lag
                if 0 <= b < PC:
                    step(b)
        wait_for(p, psend)
        wait_for(q, qsend)
        return 0

    lax.fori_loop(0, 3, apply, 0)

    result = pltpu.make_async_copy(t.at[1], out_hbm, out_sem)
    result.start()
    fs[0] = jnp.zeros((8, NP), F32)
    for k in range(3):
        fs[0, k:k + 1] = jnp.sum(fsum[k], axis=0, keepdims=True)
    for stage, there in enumerate((at_gy, at_y, at_z)):
        copies = [remote(fs.at[stage], fr.at[stage, d - 1], fsend.at[stage, d - 1], frecv.at[stage, d - 1], there(d))
                  for d in (1, 2, 3)]
        for copy in copies:
            copy.start()
        for copy in copies:
            copy.wait()
        total = fs[stage] + fr[stage, 0] + fr[stage, 1] + fr[stage, 2]
        if stage < 2:
            fs[stage + 1] = total
        else:
            forms[...] = total
    result.wait()


def in_row_order(rows, cols):
    k = jnp.arange(KT, dtype=jnp.int32)
    key = rows * KT + k
    rank = jnp.sum((key[None, :] < key[:, None]).astype(jnp.int32), axis=1)
    code = (rows * TC + cols) * KT + k
    code = jnp.sum(jnp.where(rank[None, :] == k[:, None], code[None, :], 0), axis=1)
    row = jnp.arange(TR, dtype=jnp.int32)[:, None]
    upto = jnp.sum((rows[None, :] <= row).astype(jnp.int32), axis=1)
    count = jnp.sum((rows[None, :] == row).astype(jnp.int32), axis=1)
    return code, jnp.where(count > 0, upto - 1, KT)


def body(blocks, block_rows, block_cols, probe_bits, shift):
    code, last = in_row_order(block_rows[0, 0], block_cols[0, 0])
    dma = pltpu.SemaphoreType.DMA
    out, forms = pl.pallas_call(
        kernel,
        out_shape=(
            jax.ShapeDtypeStruct((LOC, NP), F32),
            jax.ShapeDtypeStruct((8, NP), F32),
        ),
        in_specs=[
            pl.BlockSpec(memory_space=pltpu.SMEM),
            pl.BlockSpec(memory_space=pltpu.SMEM),
            pl.BlockSpec(memory_space=pl.ANY),
            pl.BlockSpec(memory_space=pltpu.VMEM),
            pl.BlockSpec(memory_space=pltpu.VMEM),
        ],
        out_specs=(
            pl.BlockSpec(memory_space=pl.ANY),
            pl.BlockSpec(memory_space=pltpu.VMEM),
        ),
        scratch_shapes=[
            pltpu.VMEM((KT, BS, BS), BF16),
            pltpu.VMEM((KT + 1, BS, NP), BF16),
            pltpu.VMEM((TC, BS, NP), BF16),
            pltpu.VMEM((2, TC, BS, NP), BF16),
            pltpu.VMEM((2, LOC, NP), F32),
            pltpu.VMEM((LOC, NP), F32),
            pltpu.VMEM((LOC, NP), F32),
            pltpu.VMEM((2, PC, 12, HB, NP), BF16),
            pltpu.VMEM((2, 2, PC, 12, HB, NP), BF16),
            pltpu.VMEM((2, PC, 6, QB, NP), BF16),
            pltpu.VMEM((2, PC, HB, NP), F32),
            pltpu.VMEM((2, 2, PC, 6, QB, NP), BF16),
            pltpu.VMEM((3, 8, NP), F32),
            pltpu.VMEM((3, 8, NP), F32),
            pltpu.VMEM((3, 3, 8, NP), F32),
            dma, dma, dma, dma,
            dma((2, 2, PC, 2, 4)),
            dma((2,)), dma((2,)), dma((2,)),
            dma((2,)), dma((2,)), dma((2, PC)),
            dma((3, 3)), dma((3, 3)),
        ],
        compiler_params=pltpu.CompilerParams(
            collective_id=0, has_side_effects=True, vmem_limit_bytes=58 * 2**20
        ),
        cost_estimate=pl.CostEstimate(
            flops=6 * KT * BS * BS * NP, bytes_accessed=18 * 2**20, transcendentals=0
        ),
    )(code, last, blocks[0, 0], probe_bits, shift.reshape(LOC // NP, NP))
    return forms[:3], out


def solution(mesh):
    return jax.shard_map(
        body,
        mesh=mesh,
        in_specs=(
            P("gy", "gx", None, None, None),
            P("gy", "gx", None),
            P("gy", "gx", None),
            P(("gy", "gx"), "gz"),
            P(("gy", "gx")),
        ),
        out_specs=(P(None, "gz"), P(("gy", "gx"), "gz")),
        check_vma=False,
    )
```

time: 512 us -> 163 us (0.32)
  blocking collectives: 219 us -> 0 us
  Pallas kernels: 0 us -> 156 us
  other arithmetic: 133 us -> 2.77 us
  local copies, waits for them, and re-layouts: 86.1 us -> 3.13 us
  matrix products: 51.5 us -> 0 us
  waiting for transfers between devices: 14.6 us -> 0 us
    all_to_all x6 -> x0, blocking collectives: 219 us -> none  [the longest x3 168 us: sum_at_owner(): lax.all_to_all(in_blocks(array, dim, count), axis, 0, 0, tiled=True)]
    pallas_call x0 -> x1, Pallas kernels: none -> 156 us  [body(): pl.pallas_call(kernel, out_shape=(jax.ShapeDtypeStruct((LOC, NP), F32), j...]
    scatter-add x3 -> x0, other arithmetic: 114 us -> none  [apply_operator(): jnp.zeros((tile_rows, block_size, probe_count), jnp.float32).at[rows_here]]
    dot_general x3 -> x0, local copies, waits for them, and re-layouts: 52.2 us -> none  [apply_operator(): jnp.einsum('kab,kbp->kap', tile_blocks, picked, preferred_element_type=jn...]
    dot_general x3 -> x0, matrix products: 51.5 us -> none  [apply_operator(): jnp.einsum('kab,kbp->kap', tile_blocks, picked, preferred_element_type=jn...]
    gather x3 -> x0, local copies, waits for them, and re-layouts: 19.7 us -> none  [apply_operator(): picked = whole[cols_here]]
    all_to_all x1 -> x0, waiting for transfers between devices: 14.6 us -> none  [copy_for_each(): return lax.all_to_all(copies, axis, split_axis=0, concat_axis=0, tiled=True)]
    convert_element_type x6 -> x0, other arithmetic: 13.9 us -> none  [the longest x3 12.3 us: apply_operator(): summed = sum_at_owner(partial_rows.astype(jnp.bfloat16), 'gx', 0)]
  transfers between devices with their start and end apart: 1 -> 0, of which waited for: 1 -> 0; matrix products, arithmetic and copies ran while one was open for 0% -> 0% of each run, Pallas kernels for 0% -> 0%
where the time goes in v1:
time: 163 us
  Pallas kernels  156 us (96%)
  local copies, waits for them, and re-layouts  3.13 us (2%)
  other arithmetic  2.77 us (2%)
    pallas_call x1, Pallas kernels, body(): pl.pallas_call(kernel, out_shape=(jax.ShapeDtypeStruct((LOC, NP), F32), j...  156 us

profile of v1, /device:TPU:0, one launch (start us, length us, event | category | flops | bytes accessed | tf_op | source)
XLA Modules:
  0.0 163.0 jit_solution(8610697399497437225)
XLA Ops:
  0.6 0.7 iota_add_fusion
  1.3 0.2 convert_reduce_fusion
  1.5 0.6 select_reduce_fusion.code
  2.1 0.8 convert_reduce_fusion.1
  2.9 0.5 compare_select_fusion.last
  3.4 156.5 %shard_map.68 = (f32[1024,128]{1,0:T(8,128)}, f32[8,128]{1,0:T(8,128)}) custom-call(s32[128]{0:T(128)} %select_reduce_fusion.code, s32[64]{0:T(128)} %compare_select_fusion.last, bf16[128,256,256]{2,1,0:T(8,128)(2,1)} %bitcast.12, s32[1024,128]{1,0:T(8,128)} %bits.1, f32[8,128]{1,0:T(8,128)} %bitcast.13), custom_call_target="tpu_custom_call" | custom-call | flops 6442450944 | bytes 18874368 | tf_op jit(solution)/shard_map/pallas_call | solution.py:257
  159.9 1.3 slice.3
  161.2 1.9 %copy.8 = f32[1024,128]{1,0:T(8,128)} copy(f32[1024,128]{1,0:T(8,128)} %get-tuple-element.13) | data formatting | bytes 1048576

commit v2 on v1

--- a/solution.py
+++ b/solution.py
@@ -16,7 +16,7 @@
 LOC = PC * BS
 F32 = jnp.float32
 BF16 = jnp.bfloat16
-UNROLL = 4
+UNROLL = 32
 
 CHUNKS = ((2, 0), (2, 1), (1, 2), (1, 3), (1, 0), (1, 1),
           (2, 2), (2, 3), (3, 0), (3, 1), (3, 2), (3, 3))
@@ -100,9 +100,9 @@
         def block(k, carry):
             acc, prev = carry
             e = code[k]
-            row = e // (KT * TC)
+            row = e >> 11
             keep = (row == prev).astype(F32)
-            prod = jnp.dot(blocks[e % KT], w[e // KT % TC], preferred_element_type=F32)
+            prod = jnp.dot(blocks[e & 127], w[(e >> 7) & 15], preferred_element_type=F32)
             acc = acc * keep + prod
             s[k] = acc.astype(BF16)
             return acc, row
@@ -235,7 +235,7 @@
         if stage < 2:
             fs[stage + 1] = total
         else:
-            forms[...] = total
+            forms[...] = total[:3]
     result.wait()
 
 
@@ -258,7 +258,7 @@
         kernel,
         out_shape=(
             jax.ShapeDtypeStruct((LOC, NP), F32),
-            jax.ShapeDtypeStruct((8, NP), F32),
+            jax.ShapeDtypeStruct((3, NP), F32),
         ),
         in_specs=[
             pl.BlockSpec(memory_space=pltpu.SMEM),
@@ -300,7 +300,7 @@
             flops=6 * KT * BS * BS * NP, bytes_accessed=18 * 2**20, transcendentals=0
         ),
     )(code, last, blocks[0, 0], probe_bits, shift.reshape(LOC // NP, NP))
-    return forms[:3], out
+    return forms, out
 
 
 def solution(mesh):

time: 163 us -> 149 us (0.914)
  Pallas kernels: 156 us -> 142 us
    pallas_call x1, Pallas kernels: 156 us -> 142 us  [body(): pl.pallas_call(kernel, out_shape=(jax.ShapeDtypeStruct((LOC, NP), F32), j...]
where the time goes in v2:
time: 149 us
  Pallas kernels  142 us (95%)
  local copies, waits for them, and re-layouts  3.13 us (2%)
  other arithmetic  2.77 us (2%)
    pallas_call x1, Pallas kernels, body(): pl.pallas_call(kernel, out_shape=(jax.ShapeDtypeStruct((LOC, NP), F32), j...  142 us
    unnamed x2, local copies, waits for them, and re-layouts  3.13 us

profile of v2, /device:TPU:0, one launch (start us, length us, event | category | flops | bytes accessed | tf_op | source)
XLA Modules:
  0.0 149.0 jit_solution(3158104784593212582)
XLA Ops:
  0.6 0.7 iota_add_fusion
  1.3 0.2 convert_reduce_fusion
  1.5 0.6 select_reduce_fusion.code
  2.1 0.8 convert_reduce_fusion.1
  2.9 0.5 compare_select_fusion.last
  3.4 142.4 %shard_map.68 = (f32[1024,128]{1,0:T(8,128)}, f32[3,128]{1,0:T(4,128)}) custom-call(s32[128]{0:T(128)} %select_reduce_fusion.code, s32[64]{0:T(128)} %compare_select_fusion.last, bf16[128,256,256]{2,1,0:T(8,128)(2,1)} %bitcast.12, s32[1024,128]{1,0:T(8,128)} %bits.1, f32[8,128]{1,0:T(8,128)} %bitcast.13), custom_call_target="tpu_custom_call" | custom-call | flops 6442450944 | bytes 18874368 | tf_op jit(solution)/shard_map/pallas_call | solution.py:257
  145.8 1.3 copy.9
  147.1 1.9 %copy.10 = f32[1024,128]{1,0:T(8,128)} copy(f32[1024,128]{1,0:T(8,128)} %get-tuple-element.13) | data formatting | bytes 1048576

commit v3 on v2

v3 whole, which is shorter than its diff:
```python
import jax
import jax.numpy as jnp
from jax import lax
from jax.experimental import pallas as pl
from jax.experimental.pallas import tpu as pltpu
from jax.sharding import PartitionSpec as P

BS = 256
KT = 128
TR = 64
TC = 16
NP = 128
NC = 2
CP = NP // NC
HP = CP // 2
RB = 4
PC = 2
G = RB // PC
LOC = RB * BS
F32 = jnp.float32
BF16 = jnp.bfloat16
UNROLL = 32

CHUNKS = ((2, 0), (2, 1), (1, 2), (1, 3), (1, 0), (1, 1),
          (2, 2), (2, 3), (3, 0), (3, 1), (3, 2), (3, 3))
FIRST = ((0, 4), (6, 4), (4, 2), (10, 2))


def kernel(code, last, blocks_hbm, bits, shift, out_hbm, forms,
           blocks, s, w, land, t, z, p, r1, q, qown, r2, fsum, fs, fr, out,
           load_sem, out_sem, psend, qsend, rs1, rs2, sib_send, part_send, fwd_send,
           sib_recv, fwd_recv, part_recv, fsend, frecv):
    gx, gy, gz = lax.axis_index("gx"), lax.axis_index("gy"), lax.axis_index("gz")
    y, zc = gx // 4, gx % 4
    sib = {"gx": gx, "gy": gy + 1 - 2 * (gy % 2), "gz": gz}
    partner_gy = (gy + 2) % 4
    part = {"gx": gx, "gy": partner_gy, "gz": gz}

    def at_y(d):
        return {"gx": (y + d) % 4 * 4 + zc, "gy": gy, "gz": gz}

    def at_z(d):
        return {"gx": y * 4 + (zc + d) % 4, "gy": gy, "gz": gz}

    def at_gy(d):
        return {"gx": gx, "gy": (gy + d) % 4, "gz": gz}

    first_axis, second_axis = (at_y, at_z), (at_z, at_y)

    load = pltpu.make_async_copy(blocks_hbm, blocks, load_sem)
    load.start()

    barrier = pltpu.get_barrier_semaphore()
    for d in (1, 2, 3):
        for there in (at_y, at_z, at_gy):
            pl.semaphore_signal(barrier, inc=1, device_id=there(d), device_id_type=pl.DeviceIdType.MESH)

    def remote(src, dst, send, recv, where):
        return pltpu.make_async_remote_copy(
            src_ref=src, dst_ref=dst, send_sem=send, recv_sem=recv,
            device_id=where, device_id_type=pl.DeviceIdType.MESH)

    def wait_for(ref, sem):
        pltpu.make_async_copy(ref, ref, sem).wait()

    for r in range(LOC // NP):
        signs = (2 * bits[r * NP:(r + 1) * NP] - 1).astype(F32).T
        b, lanes = r // 2, slice(r % 2 * NP, r % 2 * NP + NP)
        for c in range(NC):
            for h in (0, 1):
                mine = signs[(2 * c + h) * HP:(2 * c + h + 1) * HP]
                z[c, h, b, :, lanes] = mine
                t[0, c, h, b, :, lanes] = mine
                land[c, 0, gy * RB + b, h * HP:(h + 1) * HP, lanes] = mine.astype(BF16)
    t[1] = jnp.zeros_like(t[1])
    fsum[...] = jnp.zeros_like(fsum)
    for c in range(NC):
        s[c, KT] = jnp.zeros((CP, BS), BF16)

    def share(c, par, g):
        mine = land.at[c, par, pl.ds(gy * RB + g * G, G)]
        remote(mine, mine, part_send.at[c, par], part_recv.at[c, par, g], part).start()
        remote(mine, mine, sib_send.at[c, par], sib_recv.at[c, par], sib).start()

    def forward(c, par, g):
        got = land.at[c, par, pl.ds(partner_gy * RB + g * G, G)]
        wait_for(got, part_recv.at[c, par, g])
        remote(got, got, fwd_send.at[c, par], fwd_recv.at[c, par], sib).start()

    def gathered(c, par):
        four = land.at[c, par, pl.ds(0, RB)]
        for sem in (sib_recv, fwd_recv, sib_send, part_send, fwd_send):
            wait_for(four, sem.at[c, par])

    def row_of(h, b, d1, d2):
        dy, dz = (d1, d2) if h == 0 else (d2, d1)
        return last[((y + dy) % 4 * 4 + (zc + dz) % 4) * RB + b]

    def partial(c, h, b, d1, d2):
        return s[c, row_of(h, b, d1, d2), h * HP:(h + 1) * HP]

    def fill(c, h, g, m):
        at, n = FIRST[m]
        for i in range(at, at + n):
            for k in range(G):
                p[c, h, g, i, k] = partial(c, h, g * G + k, *CHUNKS[i])

    def send1(c, par, h, g, m):
        at, n = FIRST[m]
        remote(p.at[c, h, g, pl.ds(at, n)], r1.at[c, par, h, g, pl.ds(at, n)], psend.at[c],
               rs1.at[c, par, h, g, m], first_axis[h](1 if m % 2 == 0 else 3)).start()

    def arrived1(c, par, h, g, m):
        at, n = FIRST[m]
        wait_for(r1.at[c, par, h, g, pl.ds(at, n)], rs1.at[c, par, h, g, m])

    def begin(c, par):
        for g in range(PC):
            for h in (0, 1):
                for m in (0, 1):
                    fill(c, h, g, m)
                    send1(c, par, h, g, m)
        for g in range(PC):
            for h in (0, 1):
                for m in (2, 3):
                    fill(c, h, g, m)

    def hand_on(c, par, g):
        for h in (0, 1):
            for m in (0, 1):
                arrived1(c, par, h, g, m)
                to, came = FIRST[m + 2][0], FIRST[m][0]
                for i in range(2):
                    p[c, h, g, to + i] = (p[c, h, g, to + i].astype(F32)
                                          + r1[c, par, h, g, came + i].astype(F32)).astype(BF16)
                send1(c, par, h, g, m + 2)

    def second(c, par, g):
        for h in (0, 1):
            for m in (2, 3):
                arrived1(c, par, h, g, m)
            for d in (2, 1, 3, 0):
                up, down = (4 + d, 8 + d) if d < 2 else (d, 8 + d)
                for k in range(G):
                    total = (partial(c, h, g * G + k, 0, d).astype(F32)
                             + r1[c, par, h, g, up, k].astype(F32) + r1[c, par, h, g, down, k].astype(F32))
                    if d:
                        q[c, h, g, d - 1, k] = total.astype(BF16)
                    else:
                        qown[c, h, g, k] = total
                if d:
                    remote(q.at[c, h, g, d - 1], r2.at[c, par, h, g, d - 1], qsend.at[c],
                           rs2.at[c, par, h, g, d - 1], second_axis[h](d)).start()

    def finish(c, a, par, g):
        nxt = 1 - par
        factor = jnp.where(a == 0, 1.0, 2.0).astype(F32)
        for h in (0, 1):
            for d in (0, 1, 2):
                wait_for(r2.at[c, par, h, g, d], rs2.at[c, par, h, g, d])
            for k in range(G):
                b = g * G + k
                m_w = qown[c, h, g, k]
                for d in (0, 1, 2):
                    m_w = m_w + r2[c, par, h, g, d, k].astype(F32)
                new = factor * (m_w + shift[b:b + 1] * t[par, c, h, b]) - t[nxt, c, h, b]
                t[nxt, c, h, b] = new
                land[c, nxt, gy * RB + b, h * HP:(h + 1) * HP] = new.astype(BF16)
                form = z[c, h, b] * new
                fsum[a, c, h] += form[:, :NP] + form[:, NP:]

        @pl.when(a < 2)
        def _():
            share(c, nxt, g)

    def pass_on(c, a, par, g):
        @pl.when(a < 2)
        def _():
            forward(c, 1 - par, g)

    def sent(c):
        wait_for(p.at[c], psend.at[c])
        wait_for(q.at[c], qsend.at[c])

    pl.semaphore_wait(barrier, 9)
    for c in range(NC):
        for g in range(PC):
            share(c, 0, g)
    for g in range(PC):
        forward(0, 0, g)
    load.wait()

    def phase(n, _):
        c, a = n % 2, n // 2
        par = a % 2
        o, a_o = 1 - c, (n + 1) // 2 - 1
        par_o = (n + 1) // 2 % 2
        par_o = 1 - par_o
        gathered(c, par)
        w[...] = land[c, par]

        def other(step, *more):
            @pl.when(n > 0)
            def _():
                step(*more)

        def block(k, carry):
            acc, prev = carry
            e = code[k]
            row = e >> 11
            keep = (row == prev).astype(F32)
            prod = lax.dot_general(w[(e >> 7) & 15], blocks[e & 127], (((1,), (1,)), ((), ())),
                                   preferred_element_type=F32)
            acc = acc * keep + prod
            s[c, k] = acc.astype(BF16)
            return acc, row

        def group(i, carry):
            for u in range(UNROLL):
                carry = block(i * UNROLL + u, carry)
            return carry

        carry = (jnp.zeros((CP, BS), F32), jnp.int32(-1))
        other(hand_on, o, par_o, 1)
        carry = group(0, carry)
        other(second, o, par_o, 0)

        @pl.when(n == 0)
        def _():
            for g in range(PC):
                forward(1, 0, g)

        carry = group(1, carry)
        other(second, o, par_o, 1)
        carry = group(2, carry)
        other(finish, o, a_o, par_o, 0)
        carry = group(3, carry)
        begin(c, par)
        other(finish, o, a_o, par_o, 1)
        other(pass_on, o, a_o, par_o, 0)
        hand_on(c, par, 0)
        other(pass_on, o, a_o, par_o, 1)
        other(sent, o)
        return 0

    lax.fori_loop(0, 3 * NC, phase, 0)
    hand_on(1, 0, 1)
    second(1, 0, 0)
    second(1, 0, 1)
    finish(1, 2, 0, 0)
    finish(1, 2, 0, 1)
    sent(1)

    for k in range(3):
        by_probe = fsum[k].reshape(NP, NP)
        fs[0, k:k + 1] = jnp.sum(by_probe.T, axis=0, keepdims=True)
    fs[0, 3:8] = jnp.zeros((5, NP), F32)
    for stage, there in enumerate((at_gy, at_y, at_z)):
        copies = [remote(fs.at[stage], fr.at[stage, d - 1], fsend.at[stage, d - 1], frecv.at[stage, d - 1], there(d))
                  for d in (1, 2, 3)]
        for copy in copies:
            copy.start()
        if stage == 0:
            for r in range(LOC // NP):
                part_rows = t[1, :, :, r // 2, :, r % 2 * NP:r % 2 * NP + NP].reshape(NP, NP)
                out[r * NP:(r + 1) * NP] = part_rows.T
            result = pltpu.make_async_copy(out, out_hbm, out_sem)
            result.start()
        for copy in copies:
            copy.wait()
        total = fs[stage] + fr[stage, 0] + fr[stage, 1] + fr[stage, 2]
        if stage < 2:
            fs[stage + 1] = total
        else:
            forms[...] = total[:3]
    result.wait()


def in_row_order(rows, cols):
    k = jnp.arange(KT, dtype=jnp.int32)
    key = rows * KT + k
    rank = jnp.sum((key[None, :] < key[:, None]).astype(jnp.int32), axis=1)
    code = (rows * TC + cols) * KT + k
    code = jnp.sum(jnp.where(rank[None, :] == k[:, None], code[None, :], 0), axis=1)
    row = jnp.arange(TR, dtype=jnp.int32)[:, None]
    upto = jnp.sum((rows[None, :] <= row).astype(jnp.int32), axis=1)
    count = jnp.sum((rows[None, :] == row).astype(jnp.int32), axis=1)
    return code, jnp.where(count > 0, upto - 1, KT)


def body(blocks, block_rows, block_cols, probe_bits, shift):
    code, last = in_row_order(block_rows[0, 0], block_cols[0, 0])
    dma = pltpu.SemaphoreType.DMA
    out, forms = pl.pallas_call(
        kernel,
        out_shape=(
            jax.ShapeDtypeStruct((LOC, NP), F32),
            jax.ShapeDtypeStruct((3, NP), F32),
        ),
        in_specs=[
            pl.BlockSpec(memory_space=pltpu.SMEM),
            pl.BlockSpec(memory_space=pltpu.SMEM),
            pl.BlockSpec(memory_space=pl.ANY),
            pl.BlockSpec(memory_space=pltpu.VMEM),
            pl.BlockSpec(memory_space=pltpu.VMEM),
        ],
        out_specs=(
            pl.BlockSpec(memory_space=pl.ANY),
            pl.BlockSpec(memory_space=pltpu.VMEM),
        ),
        scratch_shapes=[
            pltpu.VMEM((KT, BS, BS), BF16),
            pltpu.VMEM((NC, KT + 1, CP, BS), BF16),
            pltpu.VMEM((TC, CP, BS), BF16),
            pltpu.VMEM((NC, 2, TC, CP, BS), BF16),
            pltpu.VMEM((2, NC, 2, RB, HP, BS), F32),
            pltpu.VMEM((NC, 2, RB, HP, BS), F32),
            pltpu.VMEM((NC, 2, PC, 12, G, HP, BS), BF16),
            pltpu.VMEM((NC, 2, 2, PC, 12, G, HP, BS), BF16),
            pltpu.VMEM((NC, 2, PC, 3, G, HP, BS), BF16),
            pltpu.VMEM((NC, 2, PC, G, HP, BS), F32),
            pltpu.VMEM((NC, 2, 2, PC, 3, G, HP, BS), BF16),
            pltpu.VMEM((3, NC, 2, HP, NP), F32),
            pltpu.VMEM((3, 8, NP), F32),
            pltpu.VMEM((3, 3, 8, NP), F32),
            pltpu.VMEM((LOC, NP), F32),
            dma, dma,
            dma((NC,)), dma((NC,)),
            dma((NC, 2, 2, PC, 4)),
            dma((NC, 2, 2, PC, 3)),
            dma((NC, 2)), dma((NC, 2)), dma((NC, 2)),
            dma((NC, 2)), dma((NC, 2)), dma((NC, 2, PC)),
            dma((3, 3)), dma((3, 3)),
        ],
        compiler_params=pltpu.CompilerParams(
            collective_id=0, has_side_effects=True, vmem_limit_bytes=58 * 2**20
        ),
        cost_estimate=pl.CostEstimate(
            flops=6 * KT * BS * BS * NP, bytes_accessed=18 * 2**20, transcendentals=0
        ),
    )(code, last, blocks[0, 0], probe_bits, shift.reshape(RB, BS))
    return forms, out


def solution(mesh):
    return jax.shard_map(
        body,
        mesh=mesh,
        in_specs=(
            P("gy", "gx", None, None, None),
            P("gy", "gx", None),
            P("gy", "gx", None),
            P(("gy", "gx"), "gz"),
            P(("gy", "gx")),
        ),
        out_specs=(P(None, "gz"), P(("gy", "gx"), "gz")),
        check_vma=False,
    )
```

time: 149 us -> 135 us (0.906)
  Pallas kernels: 142 us -> 127 us
    pallas_call x1, Pallas kernels: 142 us -> 127 us  [body(): pl.pallas_call(kernel, out_shape=(jax.ShapeDtypeStruct((LOC, NP), F32), j...]
where the time goes in v3:
time: 135 us
  Pallas kernels  127 us (94%)
  local copies, waits for them, and re-layouts  4.41 us (3%)
  other arithmetic  2.77 us (2%)
    pallas_call x1, Pallas kernels, body(): pl.pallas_call(kernel, out_shape=(jax.ShapeDtypeStruct((LOC, NP), F32), j...  127 us
    unnamed x2, local copies, waits for them, and re-layouts  3.13 us

profile of v3, /device:TPU:0, one launch (start us, length us, event | category | flops | bytes accessed | tf_op | source)
XLA Modules:
  0.0 134.7 jit_solution(16744310460396631909)
XLA Ops:
  0.6 0.7 iota_add_fusion
  1.3 0.2 convert_reduce_fusion
  1.5 0.6 select_reduce_fusion.code
  2.1 0.8 convert_reduce_fusion.1
  2.9 0.5 compare_select_fusion.last
  3.4 1.3 reshape.42.shift
  4.7 126.9 %shard_map.68 = (f32[1024,128]{1,0:T(8,128)}, f32[3,128]{1,0:T(4,128)}) custom-call(s32[128]{0:T(128)} %select_reduce_fusion.code, s32[64]{0:T(128)} %compare_select_fusion.last, bf16[128,256,256]{2,1,0:T(8,128)(2,1)} %bitcast.11, s32[1024,128]{1,0:T(8,128)} %bits.1, f32[4,256]{1,0:T(4,128)} %reshape.42.shift), custom_call_target="tpu_custom_call" | custom-call | flops 6442450944 | bytes 18874368 | tf_op jit(solution)/shard_map/pallas_call | solution.py:294
  131.6 1.3 copy.9
  132.8 1.9 %copy.10 = f32[1024,128]{1,0:T(8,128)} copy(f32[1024,128]{1,0:T(8,128)} %get-tuple-element.13) | data formatting | bytes 1048576

commit v4 on v3

--- a/solution.py
+++ b/solution.py
@@ -14,28 +14,27 @@
 CP = NP // NC
 HP = CP // 2
 RB = 4
-PC = 2
+PC = 4
 G = RB // PC
 LOC = RB * BS
 F32 = jnp.float32
 BF16 = jnp.bfloat16
 UNROLL = 32
+UNROLL0 = 16
+ORDER = ('h2', 'h3', 'm0', 'm1', 's0', 's1', 'm2', 's2', 's3', 'm3', 'b', 'f0', 'f1', 'f2', 'f3', 'H0', 'H1')
+FIRST_ORDER = ('H0', 'H1')
 
 CHUNKS = ((2, 0), (2, 1), (1, 2), (1, 3), (1, 0), (1, 1),
           (2, 2), (2, 3), (3, 0), (3, 1), (3, 2), (3, 3))
 FIRST = ((0, 4), (6, 4), (4, 2), (10, 2))
 
 
-def kernel(code, last, blocks_hbm, bits, shift, out_hbm, forms,
-           blocks, s, w, land, t, z, p, r1, q, qown, r2, fsum, fs, fr, out,
-           load_sem, out_sem, psend, qsend, rs1, rs2, sib_send, part_send, fwd_send,
-           sib_recv, fwd_recv, part_recv, fsend, frecv):
+def kernel(rows, cols, blocks_hbm, bits, shift, out_hbm, forms,
+           blocks, sorted_blocks, s, w, land, t, z, p, own, r1, q, qown, r2, fsum, fs, fr, out,
+           order_vmem, order, load_sem, order_sem, out_sem, psend, qsend, rs1, rs2, share_send, share_recv,
+           fsend, frecv):
     gx, gy, gz = lax.axis_index("gx"), lax.axis_index("gy"), lax.axis_index("gz")
     y, zc = gx // 4, gx % 4
-    sib = {"gx": gx, "gy": gy + 1 - 2 * (gy % 2), "gz": gz}
-    partner_gy = (gy + 2) % 4
-    part = {"gx": gx, "gy": partner_gy, "gz": gz}
-
     def at_y(d):
         return {"gx": (y + d) % 4 * 4 + zc, "gy": gy, "gz": gz}
 
@@ -43,7 +42,8 @@
         return {"gx": y * 4 + (zc + d) % 4, "gy": gy, "gz": gz}
 
     def at_gy(d):
-        return {"gx": gx, "gy": (gy + d) % 4, "gz": gz}
+        other_core = gy + 1 - 2 * (gy % 2)
+        return {"gx": gx, "gy": ((gy if d == 2 else other_core) + (2 if d > 1 else 0)) % 4, "gz": gz}
 
     first_axis, second_axis = (at_y, at_z), (at_z, at_y)
 
@@ -74,36 +74,47 @@
                 land[c, 0, gy * RB + b, h * HP:(h + 1) * HP, lanes] = mine.astype(BF16)
     t[1] = jnp.zeros_like(t[1])
     fsum[...] = jnp.zeros_like(fsum)
-    for c in range(NC):
-        s[c, KT] = jnp.zeros((CP, BS), BF16)
+    s[KT] = jnp.zeros((CP, BS), BF16)
+
+    lane = lax.broadcasted_iota(jnp.int32, (KT, KT), 1)
+    stored = lax.broadcasted_iota(jnp.int32, (KT, KT), 0)
+    rows_across = jnp.broadcast_to(rows[...], (KT, KT))
+    rows_down = rows_across.astype(F32).T.astype(jnp.int32)
+    cols_down = jnp.broadcast_to(cols[...], (KT, KT)).astype(F32).T.astype(jnp.int32)
+    before = rows_across * KT + lane < rows_down * KT + stored
+    rank = jnp.sum(before.astype(jnp.int32), axis=1, keepdims=True)
+    entry = (rows_down * TC + cols_down) * KT + stored
+    order_vmem[...] = jnp.zeros_like(order_vmem)
+    order_vmem[0:1] = jnp.sum(jnp.where(rank == lane, entry, 0), axis=0, keepdims=True)
+    upto = jnp.sum((rows_down <= lane).astype(jnp.int32), axis=0, keepdims=True)
+    held = jnp.sum((rows_down == lane).astype(jnp.int32), axis=0, keepdims=True)
+    order_vmem[1:2] = jnp.where(held > 0, upto - 1, KT)
+    ordering = pltpu.make_async_copy(order_vmem, order, order_sem)
+    ordering.start()
 
     def share(c, par, g):
         mine = land.at[c, par, pl.ds(gy * RB + g * G, G)]
-        remote(mine, mine, part_send.at[c, par], part_recv.at[c, par, g], part).start()
-        remote(mine, mine, sib_send.at[c, par], sib_recv.at[c, par], sib).start()
-
-    def forward(c, par, g):
-        got = land.at[c, par, pl.ds(partner_gy * RB + g * G, G)]
-        wait_for(got, part_recv.at[c, par, g])
-        remote(got, got, fwd_send.at[c, par], fwd_recv.at[c, par], sib).start()
+        for d in (2, 1, 3):
+            remote(mine, mine, share_send.at[c, par, d - 1], share_recv.at[c, par, d - 1], at_gy(d)).start()
 
     def gathered(c, par):
         four = land.at[c, par, pl.ds(0, RB)]
-        for sem in (sib_recv, fwd_recv, sib_send, part_send, fwd_send):
-            wait_for(four, sem.at[c, par])
+        for sem in (share_recv, share_send):
+            for d in (1, 2, 3):
+                wait_for(four, sem.at[c, par, d - 1])
 
     def row_of(h, b, d1, d2):
         dy, dz = (d1, d2) if h == 0 else (d2, d1)
-        return last[((y + dy) % 4 * 4 + (zc + dz) % 4) * RB + b]
-
-    def partial(c, h, b, d1, d2):
-        return s[c, row_of(h, b, d1, d2), h * HP:(h + 1) * HP]
+        return order[1, ((y + dy) % 4 * 4 + (zc + dz) % 4) * RB + b]
+
+    def partial(h, b, d1, d2):
+        return s[row_of(h, b, d1, d2), h * HP:(h + 1) * HP]
 
     def fill(c, h, g, m):
         at, n = FIRST[m]
         for i in range(at, at + n):
             for k in range(G):
-                p[c, h, g, i, k] = partial(c, h, g * G + k, *CHUNKS[i])
+                p[c, h, g, i, k] = partial(h, g * G + k, *CHUNKS[i])
 
     def send1(c, par, h, g, m):
         at, n = FIRST[m]
@@ -124,6 +135,9 @@
             for h in (0, 1):
                 for m in (2, 3):
                     fill(c, h, g, m)
+                for d in range(4):
+                    for k in range(G):
+                        own[c, h, g, d, k] = partial(h, g * G + k, 0, d)
 
     def hand_on(c, par, g):
         for h in (0, 1):
@@ -142,7 +156,7 @@
             for d in (2, 1, 3, 0):
                 up, down = (4 + d, 8 + d) if d < 2 else (d, 8 + d)
                 for k in range(G):
-                    total = (partial(c, h, g * G + k, 0, d).astype(F32)
+                    total = (own[c, h, g, d, k].astype(F32)
                              + r1[c, par, h, g, up, k].astype(F32) + r1[c, par, h, g, down, k].astype(F32))
                     if d:
                         q[c, h, g, d - 1, k] = total.astype(BF16)
@@ -173,11 +187,6 @@
         def _():
             share(c, nxt, g)
 
-    def pass_on(c, a, par, g):
-        @pl.when(a < 2)
-        def _():
-            forward(c, 1 - par, g)
-
     def sent(c):
         wait_for(p.at[c], psend.at[c])
         wait_for(q.at[c], qsend.at[c])
@@ -186,69 +195,68 @@
     for c in range(NC):
         for g in range(PC):
             share(c, 0, g)
-    for g in range(PC):
-        forward(0, 0, g)
+    ordering.wait()
     load.wait()
+
+    steps = {
+        "h": lambda c, a, par, g: hand_on(c, par, g),
+        "s": lambda c, a, par, g: second(c, par, g),
+        "f": finish,
+    }
+
+    def block(k, carry, first):
+        acc, prev = carry
+        e = order[0, k]
+        row = e >> 11
+        keep = (row == prev).astype(F32)
+        if first:
+            columns = blocks[e & 127].T
+            sorted_blocks[k] = columns
+        else:
+            columns = sorted_blocks[k]
+        acc = acc * keep + jnp.dot(w[(e >> 7) & 15], columns, preferred_element_type=F32)
+        s[k] = acc.astype(BF16)
+        return acc, row
+
+    def group(i, carry, first=False):
+        per = UNROLL0 if first else UNROLL
+        for u in range(per):
+            carry = block(i * per + u, carry, first)
+        return carry
+
+    start = (jnp.zeros((CP, BS), F32), jnp.int32(-1))
+    gathered(0, 0)
+    w[...] = land[0, 0]
+    lax.fori_loop(0, KT // UNROLL0, lambda i, carry: group(i, carry, True), start)
+    begin(0, 0)
+    for token in FIRST_ORDER:
+        steps[token[0].lower()](0, 0, 0, int(token[1:]))
 
     def phase(n, _):
         c, a = n % 2, n // 2
         par = a % 2
-        o, a_o = 1 - c, (n + 1) // 2 - 1
-        par_o = (n + 1) // 2 % 2
-        par_o = 1 - par_o
+        o, a_o = 1 - c, (n - 1) // 2
+        par_o = a_o % 2
         gathered(c, par)
         w[...] = land[c, par]
-
-        def other(step, *more):
-            @pl.when(n > 0)
-            def _():
-                step(*more)
-
-        def block(k, carry):
-            acc, prev = carry
-            e = code[k]
-            row = e >> 11
-            keep = (row == prev).astype(F32)
-            prod = lax.dot_general(w[(e >> 7) & 15], blocks[e & 127], (((1,), (1,)), ((), ())),
-                                   preferred_element_type=F32)
-            acc = acc * keep + prod
-            s[c, k] = acc.astype(BF16)
-            return acc, row
-
-        def group(i, carry):
-            for u in range(UNROLL):
-                carry = block(i * UNROLL + u, carry)
-            return carry
-
-        carry = (jnp.zeros((CP, BS), F32), jnp.int32(-1))
-        other(hand_on, o, par_o, 1)
-        carry = group(0, carry)
-        other(second, o, par_o, 0)
-
-        @pl.when(n == 0)
-        def _():
-            for g in range(PC):
-                forward(1, 0, g)
-
-        carry = group(1, carry)
-        other(second, o, par_o, 1)
-        carry = group(2, carry)
-        other(finish, o, a_o, par_o, 0)
-        carry = group(3, carry)
-        begin(c, par)
-        other(finish, o, a_o, par_o, 1)
-        other(pass_on, o, a_o, par_o, 0)
-        hand_on(c, par, 0)
-        other(pass_on, o, a_o, par_o, 1)
-        other(sent, o)
+        carry = start
+        for token in ORDER:
+            what, g = token[0], int(token[1:] or 0)
+            if what == "m":
+                carry = group(g, carry)
+            elif what == "b":
+                begin(c, par)
+            elif what in "HSF":
+                steps[what.lower()](c, a, par, g)
+            else:
+                steps[what](o, a_o, par_o, g)
+        sent(o)
         return 0
 
-    lax.fori_loop(0, 3 * NC, phase, 0)
-    hand_on(1, 0, 1)
-    second(1, 0, 0)
-    second(1, 0, 1)
-    finish(1, 2, 0, 0)
-    finish(1, 2, 0, 1)
+    lax.fori_loop(1, 3 * NC, phase, 0)
+    for token in ORDER:
+        if token[0] in "hsf":
+            steps[token[0]](1, 2, 0, int(token[1:]))
     sent(1)
 
     for k in range(3):
@@ -276,20 +284,7 @@
     result.wait()
 
 
-def in_row_order(rows, cols):
-    k = jnp.arange(KT, dtype=jnp.int32)
-    key = rows * KT + k
-    rank = jnp.sum((key[None, :] < key[:, None]).astype(jnp.int32), axis=1)
-    code = (rows * TC + cols) * KT + k
-    code = jnp.sum(jnp.where(rank[None, :] == k[:, None], code[None, :], 0), axis=1)
-    row = jnp.arange(TR, dtype=jnp.int32)[:, None]
-    upto = jnp.sum((rows[None, :] <= row).astype(jnp.int32), axis=1)
-    count = jnp.sum((rows[None, :] == row).astype(jnp.int32), axis=1)
-    return code, jnp.where(count > 0, upto - 1, KT)
-
-
 def body(blocks, block_rows, block_cols, probe_bits, shift):
-    code, last = in_row_order(block_rows[0, 0], block_cols[0, 0])
     dma = pltpu.SemaphoreType.DMA
     out, forms = pl.pallas_call(
         kernel,
@@ -298,8 +293,8 @@
             jax.ShapeDtypeStruct((3, NP), F32),
         ),
         in_specs=[
-            pl.BlockSpec(memory_space=pltpu.SMEM),
-            pl.BlockSpec(memory_space=pltpu.SMEM),
+            pl.BlockSpec(memory_space=pltpu.VMEM),
+            pl.BlockSpec(memory_space=pltpu.VMEM),
             pl.BlockSpec(memory_space=pl.ANY),
             pl.BlockSpec(memory_space=pltpu.VMEM),
             pl.BlockSpec(memory_space=pltpu.VMEM),
@@ -310,12 +305,14 @@
         ),
         scratch_shapes=[
             pltpu.VMEM((KT, BS, BS), BF16),
-            pltpu.VMEM((NC, KT + 1, CP, BS), BF16),
+            pltpu.VMEM((KT, BS, BS), BF16),
+            pltpu.VMEM((KT + 1, CP, BS), BF16),
             pltpu.VMEM((TC, CP, BS), BF16),
             pltpu.VMEM((NC, 2, TC, CP, BS), BF16),
             pltpu.VMEM((2, NC, 2, RB, HP, BS), F32),
             pltpu.VMEM((NC, 2, RB, HP, BS), F32),
             pltpu.VMEM((NC, 2, PC, 12, G, HP, BS), BF16),
+            pltpu.VMEM((NC, 2, PC, 4, G, HP, BS), BF16),
             pltpu.VMEM((NC, 2, 2, PC, 12, G, HP, BS), BF16),
             pltpu.VMEM((NC, 2, PC, 3, G, HP, BS), BF16),
             pltpu.VMEM((NC, 2, PC, G, HP, BS), F32),
@@ -324,21 +321,22 @@
             pltpu.VMEM((3, 8, NP), F32),
             pltpu.VMEM((3, 3, 8, NP), F32),
             pltpu.VMEM((LOC, NP), F32),
-            dma, dma,
+            pltpu.VMEM((8, KT), jnp.int32),
+            pltpu.SMEM((8, KT), jnp.int32),
+            dma, dma, dma,
             dma((NC,)), dma((NC,)),
             dma((NC, 2, 2, PC, 4)),
             dma((NC, 2, 2, PC, 3)),
-            dma((NC, 2)), dma((NC, 2)), dma((NC, 2)),
-            dma((NC, 2)), dma((NC, 2)), dma((NC, 2, PC)),
+            dma((NC, 2, 3)), dma((NC, 2, 3)),
             dma((3, 3)), dma((3, 3)),
         ],
         compiler_params=pltpu.CompilerParams(
-            collective_id=0, has_side_effects=True, vmem_limit_bytes=58 * 2**20
+            collective_id=0, has_side_effects=True, vmem_limit_bytes=60 * 2**20
         ),
         cost_estimate=pl.CostEstimate(
             flops=6 * KT * BS * BS * NP, bytes_accessed=18 * 2**20, transcendentals=0
         ),
-    )(code, last, blocks[0, 0], probe_bits, shift.reshape(RB, BS))
+    )(block_rows[0], block_cols[0], blocks[0, 0], probe_bits, shift.reshape(RB, BS))
     return forms, out
 
 

time: 135 us -> 124 us (0.919)
  Pallas kernels: 127 us -> 119 us
  other arithmetic: 2.77 us -> 0 us
    pallas_call x1, Pallas kernels: 127 us -> 119 us  [body(): pl.pallas_call(kernel, out_shape=(jax.ShapeDtypeStruct((LOC, NP), F32), j...]
    reduce_sum x3 -> x0, other arithmetic: 1.57 us -> none  [the longest x1 0.76 us: in_row_order(): upto = jnp.sum((rows[None, :] <= row).astype(jnp.int32), axis=1)]
where the time goes in v4:
time: 124 us
  Pallas kernels  119 us (96%)
  local copies, waits for them, and re-layouts  4.41 us (4%)
    pallas_call x1, Pallas kernels, body(): pl.pallas_call(kernel, out_shape=(jax.ShapeDtypeStruct((LOC, NP), F32), j...  119 us
    unnamed x2, local copies, waits for them, and re-layouts  3.12 us

profile of v4, /device:TPU:0, one launch (start us, length us, event | category | flops | bytes accessed | tf_op | source)
XLA Modules:
  0.0 123.9 jit_solution(8717858428191268248)
XLA Ops:
  0.6 1.3 %reshape.7.shift = f32[4,256]{1,0:T(4,128)} reshape(f32[1024]{0:T(1024)} %param.9) | data formatting | bytes 8192 | tf_op jit(solution)/shard_map/reshape | solution.py:339
  1.9 118.8 %shard_map.68 = (f32[1024,128]{1,0:T(8,128)}, f32[3,128]{1,0:T(4,128)}) custom-call(s32[1,128]{1,0:T(1,128)} %bitcast.4, s32[1,128]{1,0:T(1,128)} %bitcast.5, bf16[128,256,256]{2,1,0:T(8,128)(2,1)} %bitcast.3, s32[1024,128]{1,0:T(8,128)} %bits.1, f32[4,256]{1,0:T(4,128)} %reshape.7.shift), custom_call_target="tpu_custom_call" | custom-call | flops 6442450944 | bytes 18874368 | tf_op jit(solution)/shard_map/pallas_call | solution.py:289
  120.7 1.3 %copy.9 = f32[3,128]{1,0:T(4,128)} copy(f32[3,128]{1,0:T(4,128)} %get-tuple-element.8) | data formatting | bytes 3072
  122.0 1.9 %copy.10 = f32[1024,128]{1,0:T(8,128)} copy(f32[1024,128]{1,0:T(8,128)} %get-tuple-element.9) | data formatting | bytes 1048576

commit v5 on v4

--- a/solution.py
+++ b/solution.py
@@ -20,9 +20,9 @@
 F32 = jnp.float32
 BF16 = jnp.bfloat16
 UNROLL = 32
-UNROLL0 = 16
-ORDER = ('h2', 'h3', 'm0', 'm1', 's0', 's1', 'm2', 's2', 's3', 'm3', 'b', 'f0', 'f1', 'f2', 'f3', 'H0', 'H1')
-FIRST_ORDER = ('H0', 'H1')
+LOAD = 16
+ORDER = ('w.0', 'm0.0', 's0.1', 'm1.0', 's1.1', 'm2.0', 's2.1', 'm3.0', 's3.1', 'b.0', 'f0.1', 'f1.1', 'f2.1', 'f3.1', 'e.1', 'h0.0', 'h1.0', 'h2.0', 'h3.0')
+
 
 CHUNKS = ((2, 0), (2, 1), (1, 2), (1, 3), (1, 0), (1, 1),
           (2, 2), (2, 3), (3, 0), (3, 1), (3, 2), (3, 3))
@@ -30,7 +30,7 @@
 
 
 def kernel(rows, cols, blocks_hbm, bits, shift, out_hbm, forms,
-           blocks, sorted_blocks, s, w, land, t, z, p, own, r1, q, qown, r2, fsum, fs, fr, out,
+           blocks, s, w, land, t, z, p, own, r1, q, qown, r2, fsum, fs, fr, out,
            order_vmem, order, load_sem, order_sem, out_sem, psend, qsend, rs1, rs2, share_send, share_recv,
            fsend, frecv):
     gx, gy, gz = lax.axis_index("gx"), lax.axis_index("gy"), lax.axis_index("gz")
@@ -47,8 +47,12 @@
 
     first_axis, second_axis = (at_y, at_z), (at_z, at_y)
 
-    load = pltpu.make_async_copy(blocks_hbm, blocks, load_sem)
-    load.start()
+    def load(i):
+        part = pl.ds(i * LOAD, LOAD)
+        return pltpu.make_async_copy(blocks_hbm.at[part], blocks.at[part], load_sem.at[i])
+
+    for i in range(KT // LOAD):
+        load(i).start()
 
     barrier = pltpu.get_barrier_semaphore()
     for d in (1, 2, 3):
@@ -196,68 +200,67 @@
         for g in range(PC):
             share(c, 0, g)
     ordering.wait()
-    load.wait()
-
-    steps = {
-        "h": lambda c, a, par, g: hand_on(c, par, g),
-        "s": lambda c, a, par, g: second(c, par, g),
-        "f": finish,
-    }
-
-    def block(k, carry, first):
+
+    def turn(i, _):
+        load(i).wait()
+        for u in range(LOAD):
+            blocks[i * LOAD + u] = blocks[i * LOAD + u].T
+        return 0
+
+    lax.fori_loop(0, KT // LOAD, turn, 0)
+
+    def block(k, carry):
         acc, prev = carry
         e = order[0, k]
         row = e >> 11
         keep = (row == prev).astype(F32)
-        if first:
-            columns = blocks[e & 127].T
-            sorted_blocks[k] = columns
-        else:
-            columns = sorted_blocks[k]
-        acc = acc * keep + jnp.dot(w[(e >> 7) & 15], columns, preferred_element_type=F32)
+        acc = acc * keep + jnp.dot(w[(e >> 7) & 15], blocks[e & 127], preferred_element_type=F32)
         s[k] = acc.astype(BF16)
         return acc, row
 
-    def group(i, carry, first=False):
-        per = UNROLL0 if first else UNROLL
-        for u in range(per):
-            carry = block(i * per + u, carry, first)
+    def group(i, carry):
+        for u in range(UNROLL):
+            carry = block(i * UNROLL + u, carry)
         return carry
 
-    start = (jnp.zeros((CP, BS), F32), jnp.int32(-1))
-    gathered(0, 0)
-    w[...] = land[0, 0]
-    lax.fori_loop(0, KT // UNROLL0, lambda i, carry: group(i, carry, True), start)
-    begin(0, 0)
-    for token in FIRST_ORDER:
-        steps[token[0].lower()](0, 0, 0, int(token[1:]))
-
-    def phase(n, _):
-        c, a = n % 2, n // 2
-        par = a % 2
-        o, a_o = 1 - c, (n - 1) // 2
-        par_o = a_o % 2
+    def take(c, par):
         gathered(c, par)
         w[...] = land[c, par]
-        carry = start
+
+    steps = {
+        "w": lambda c, a, par, g: take(c, par),
+        "b": lambda c, a, par, g: begin(c, par),
+        "h": lambda c, a, par, g: hand_on(c, par, g),
+        "s": lambda c, a, par, g: second(c, par, g),
+        "f": finish,
+        "e": lambda c, a, par, g: sent(c),
+    }
+
+    def do(token, n):
+        step, lag = token.split(".")
+        m = n - int(lag)
+        steps[step[0]](m % NC, m // NC, m // NC % 2, int(step[1:] or 0))
+
+    def phase(n, _):
+        carry = (jnp.zeros((CP, BS), F32), jnp.int32(-1))
         for token in ORDER:
-            what, g = token[0], int(token[1:] or 0)
-            if what == "m":
-                carry = group(g, carry)
-            elif what == "b":
-                begin(c, par)
-            elif what in "HSF":
-                steps[what.lower()](c, a, par, g)
+            lag = int(token.split(".")[1])
+            if token[0] == "m":
+                carry = group(int(token[1:-2]), carry)
+            elif lag == 0:
+                do(token, n)
             else:
-                steps[what](o, a_o, par_o, g)
-        sent(o)
+                @pl.when(n >= lag)
+                def _():
+                    do(token, n)
         return 0
 
-    lax.fori_loop(1, 3 * NC, phase, 0)
-    for token in ORDER:
-        if token[0] in "hsf":
-            steps[token[0]](1, 2, 0, int(token[1:]))
-    sent(1)
+    phases = 3 * NC
+    lax.fori_loop(0, phases, phase, 0)
+    for n in range(phases, phases + NC):
+        for token in ORDER:
+            if n - int(token.split(".")[1]) < phases and token[0] != "m":
+                do(token, n)
 
     for k in range(3):
         by_probe = fsum[k].reshape(NP, NP)
@@ -305,7 +308,6 @@
         ),
         scratch_shapes=[
             pltpu.VMEM((KT, BS, BS), BF16),
-            pltpu.VMEM((KT, BS, BS), BF16),
             pltpu.VMEM((KT + 1, CP, BS), BF16),
             pltpu.VMEM((TC, CP, BS), BF16),
             pltpu.VMEM((NC, 2, TC, CP, BS), BF16),
@@ -323,7 +325,7 @@
             pltpu.VMEM((LOC, NP), F32),
             pltpu.VMEM((8, KT), jnp.int32),
             pltpu.SMEM((8, KT), jnp.int32),
-            dma, dma, dma,
+            dma((KT // LOAD,)), dma, dma,
             dma((NC,)), dma((NC,)),
             dma((NC, 2, 2, PC, 4)),
             dma((NC, 2, 2, PC, 3)),

time: 124 us -> 120 us (0.968)
  Pallas kernels: 119 us -> 115 us
    pallas_call x1, Pallas kernels: 119 us -> 115 us  [body(): pl.pallas_call(kernel, out_shape=(jax.ShapeDtypeStruct((LOC, NP), F32), j...]
where the time goes in v5:
time: 120 us
  Pallas kernels  115 us (96%)
  local copies, waits for them, and re-layouts  4.41 us (4%)
    pallas_call x1, Pallas kernels, body(): pl.pallas_call(kernel, out_shape=(jax.ShapeDtypeStruct((LOC, NP), F32), j...  115 us
    unnamed x2, local copies, waits for them, and re-layouts  3.12 us

profile of v5, /device:TPU:0, one launch (start us, length us, event | category | flops | bytes accessed | tf_op | source)
XLA Modules:
  0.0 119.6 jit_solution(8446155765644904963)
XLA Ops:
  0.6 1.3 %reshape.7.shift = f32[4,256]{1,0:T(4,128)} reshape(f32[1024]{0:T(1024)} %param.9) | data formatting | bytes 8192 | tf_op jit(solution)/shard_map/reshape | solution.py:341
  1.9 114.6 %shard_map.68 = (f32[1024,128]{1,0:T(8,128)}, f32[3,128]{1,0:T(4,128)}) custom-call(s32[1,128]{1,0:T(1,128)} %bitcast.4, s32[1,128]{1,0:T(1,128)} %bitcast.5, bf16[128,256,256]{2,1,0:T(8,128)(2,1)} %bitcast.3, s32[1024,128]{1,0:T(8,128)} %bits.1, f32[4,256]{1,0:T(4,128)} %reshape.7.shift), custom_call_target="tpu_custom_call" | custom-call | flops 6442450944 | bytes 18874368 | tf_op jit(solution)/shard_map/pallas_call | solution.py:292
  116.5 1.3 %copy.9 = f32[3,128]{1,0:T(4,128)} copy(f32[3,128]{1,0:T(4,128)} %get-tuple-element.8) | data formatting | bytes 3072
  117.8 1.9 %copy.10 = f32[1024,128]{1,0:T(8,128)} copy(f32[1024,128]{1,0:T(8,128)} %get-tuple-element.9) | data formatting | bytes 1048576

commit v6 on v5

--- a/solution.py
+++ b/solution.py
@@ -30,8 +30,8 @@
 
 
 def kernel(rows, cols, blocks_hbm, bits, shift, out_hbm, forms,
-           blocks, s, w, land, t, z, p, own, r1, q, qown, r2, fsum, fs, fr, out,
-           order_vmem, order, load_sem, order_sem, out_sem, psend, qsend, rs1, rs2, share_send, share_recv,
+           blocks, s, w, land, t, z, zb, zg, p, own, r1, q, qown, r2, fsum, fs, fr, out,
+           order_vmem, order, load_sem, order_sem, out_sem, psend, qsend, zsend, zrecv, rs1, rs2, share_send, share_recv,
            fsend, frecv):
     gx, gy, gz = lax.axis_index("gx"), lax.axis_index("gy"), lax.axis_index("gz")
     y, zc = gx // 4, gx % 4
@@ -74,6 +74,7 @@
             for h in (0, 1):
                 mine = signs[(2 * c + h) * HP:(2 * c + h + 1) * HP]
                 z[c, h, b, :, lanes] = mine
+                zb[c, h, b, :, lanes] = mine.astype(BF16)
                 t[0, c, h, b, :, lanes] = mine
                 land[c, 0, gy * RB + b, h * HP:(h + 1) * HP, lanes] = mine.astype(BF16)
     t[1] = jnp.zeros_like(t[1])
@@ -153,8 +154,12 @@
                                           + r1[c, par, h, g, came + i].astype(F32)).astype(BF16)
                 send1(c, par, h, g, m + 2)
 
-    def second(c, par, g):
+    def scale(a):
+        return jnp.where(a == 0, 1.0, 2.0).astype(F32)
+
+    def second(c, a, par, g):
         for h in (0, 1):
+            form = jnp.zeros((HP, BS), F32)
             for m in (2, 3):
                 arrived1(c, par, h, g, m)
             for d in (2, 1, 3, 0):
@@ -162,17 +167,21 @@
                 for k in range(G):
                     total = (own[c, h, g, d, k].astype(F32)
                              + r1[c, par, h, g, up, k].astype(F32) + r1[c, par, h, g, down, k].astype(F32))
+                    b = g * G + k
                     if d:
                         q[c, h, g, d - 1, k] = total.astype(BF16)
+                        form = form + zg[c, h, d - 1, b].astype(F32) * (scale(a) * total)
                     else:
                         qown[c, h, g, k] = total
+                        form = form + z[c, h, b] * (scale(a) * (total + shift[b:b + 1] * t[par, c, h, b])
+                                                    - t[1 - par, c, h, b])
                 if d:
                     remote(q.at[c, h, g, d - 1], r2.at[c, par, h, g, d - 1], qsend.at[c],
                            rs2.at[c, par, h, g, d - 1], second_axis[h](d)).start()
+            fsum[a, c, h] += form[:, :NP] + form[:, NP:]
 
     def finish(c, a, par, g):
         nxt = 1 - par
-        factor = jnp.where(a == 0, 1.0, 2.0).astype(F32)
         for h in (0, 1):
             for d in (0, 1, 2):
                 wait_for(r2.at[c, par, h, g, d], rs2.at[c, par, h, g, d])
@@ -181,11 +190,9 @@
                 m_w = qown[c, h, g, k]
                 for d in (0, 1, 2):
                     m_w = m_w + r2[c, par, h, g, d, k].astype(F32)
-                new = factor * (m_w + shift[b:b + 1] * t[par, c, h, b]) - t[nxt, c, h, b]
+                new = scale(a) * (m_w + shift[b:b + 1] * t[par, c, h, b]) - t[nxt, c, h, b]
                 t[nxt, c, h, b] = new
                 land[c, nxt, gy * RB + b, h * HP:(h + 1) * HP] = new.astype(BF16)
-                form = z[c, h, b] * new
-                fsum[a, c, h] += form[:, :NP] + form[:, NP:]
 
         @pl.when(a < 2)
         def _():
@@ -199,6 +206,10 @@
     for c in range(NC):
         for g in range(PC):
             share(c, 0, g)
+    for d in (1, 3, 2):
+        for c in range(NC):
+            for h in (0, 1):
+                remote(zb.at[c, h], zg.at[c, h, 3 - d], zsend, zrecv, second_axis[h](d)).start()
     ordering.wait()
 
     def turn(i, _):
@@ -231,7 +242,7 @@
         "w": lambda c, a, par, g: take(c, par),
         "b": lambda c, a, par, g: begin(c, par),
         "h": lambda c, a, par, g: hand_on(c, par, g),
-        "s": lambda c, a, par, g: second(c, par, g),
+        "s": second,
         "f": finish,
         "e": lambda c, a, par, g: sent(c),
     }
@@ -242,6 +253,11 @@
         steps[step[0]](m % NC, m // NC, m // NC % 2, int(step[1:] or 0))
 
     def phase(n, _):
+        @pl.when(n == 1)
+        def _():
+            wait_for(zg, zrecv)
+            wait_for(zg, zsend)
+
         carry = (jnp.zeros((CP, BS), F32), jnp.int32(-1))
         for token in ORDER:
             lag = int(token.split(".")[1])
@@ -257,33 +273,43 @@
 
     phases = 3 * NC
     lax.fori_loop(0, phases, phase, 0)
-    for n in range(phases, phases + NC):
-        for token in ORDER:
-            if n - int(token.split(".")[1]) < phases and token[0] != "m":
-                do(token, n)
-
+
+    def exchange(stage):
+        there = (at_gy, at_y, at_z)[stage]
+        return [remote(fs.at[stage], fr.at[stage, d - 1], fsend.at[stage, d - 1], frecv.at[stage, d - 1], there(d))
+                for d in (2, 1, 3)]
+
+    def total_of(stage):
+        for copy in exchange(stage):
+            copy.wait()
+        return fs[stage] + fr[stage, 0] + fr[stage, 1] + fr[stage, 2]
+
+    def go(stage):
+        for copy in exchange(stage):
+            copy.start()
+
+    final = NC - 1
+    for g in range(PC):
+        second(final, 2, 0, g)
+    fs[0] = jnp.zeros((8, NP), F32)
     for k in range(3):
-        by_probe = fsum[k].reshape(NP, NP)
-        fs[0, k:k + 1] = jnp.sum(by_probe.T, axis=0, keepdims=True)
-    fs[0, 3:8] = jnp.zeros((5, NP), F32)
-    for stage, there in enumerate((at_gy, at_y, at_z)):
-        copies = [remote(fs.at[stage], fr.at[stage, d - 1], fsend.at[stage, d - 1], frecv.at[stage, d - 1], there(d))
-                  for d in (1, 2, 3)]
-        for copy in copies:
-            copy.start()
-        if stage == 0:
-            for r in range(LOC // NP):
-                part_rows = t[1, :, :, r // 2, :, r % 2 * NP:r % 2 * NP + NP].reshape(NP, NP)
-                out[r * NP:(r + 1) * NP] = part_rows.T
-            result = pltpu.make_async_copy(out, out_hbm, out_sem)
-            result.start()
-        for copy in copies:
-            copy.wait()
-        total = fs[stage] + fr[stage, 0] + fr[stage, 1] + fr[stage, 2]
-        if stage < 2:
-            fs[stage + 1] = total
-        else:
-            forms[...] = total[:3]
+        fs[0, k:k + 1] = jnp.sum(fsum[k].reshape(NP, NP).T, axis=0, keepdims=True)
+    go(0)
+    finish(final, 2, 0, 0)
+    finish(final, 2, 0, 1)
+    fs[1] = total_of(0)
+    go(1)
+    for g in range(2, PC):
+        finish(final, 2, 0, g)
+    for r in range(LOC // NP):
+        part_rows = t[1, :, :, r // 2, :, r % 2 * NP:r % 2 * NP + NP].reshape(NP, NP)
+        out[r * NP:(r + 1) * NP] = part_rows.T
+    result = pltpu.make_async_copy(out, out_hbm, out_sem)
+    result.start()
+    sent(final)
+    fs[2] = total_of(1)
+    go(2)
+    forms[...] = total_of(2)[:3]
     result.wait()
 
 
@@ -313,6 +339,8 @@
             pltpu.VMEM((NC, 2, TC, CP, BS), BF16),
             pltpu.VMEM((2, NC, 2, RB, HP, BS), F32),
             pltpu.VMEM((NC, 2, RB, HP, BS), F32),
+            pltpu.VMEM((NC, 2, RB, HP, BS), BF16),
+            pltpu.VMEM((NC, 2, 3, RB, HP, BS), BF16),
             pltpu.VMEM((NC, 2, PC, 12, G, HP, BS), BF16),
             pltpu.VMEM((NC, 2, PC, 4, G, HP, BS), BF16),
             pltpu.VMEM((NC, 2, 2, PC, 12, G, HP, BS), BF16),
@@ -327,6 +355,7 @@
             pltpu.SMEM((8, KT), jnp.int32),
             dma((KT // LOAD,)), dma, dma,
             dma((NC,)), dma((NC,)),
+            dma, dma,
             dma((NC, 2, 2, PC, 4)),
             dma((NC, 2, 2, PC, 3)),
             dma((NC, 2, 3)), dma((NC, 2, 3)),

time: 120 us -> 117 us (0.975)
  Pallas kernels: 115 us -> 111 us
    pallas_call x1, Pallas kernels: 115 us -> 111 us  [body(): pl.pallas_call(kernel, out_shape=(jax.ShapeDtypeStruct((LOC, NP), F32), j...]
where the time goes in v6:
time: 117 us; the launch traced here: 116 us
  Pallas kernels  111 us (95%)
  local copies, waits for them, and re-layouts  4.41 us (4%)
    pallas_call x1, Pallas kernels, body(): pl.pallas_call(kernel, out_shape=(jax.ShapeDtypeStruct((LOC, NP), F32), j...  111 us
    unnamed x2, local copies, waits for them, and re-layouts  3.12 us

profile of v6, /device:TPU:0, one launch (start us, length us, event | category | flops | bytes accessed | tf_op | source)
XLA Modules:
  0.0 116.5 jit_solution(10382877431982101502)
XLA Ops:
  0.6 1.3 %reshape.7.shift = f32[4,256]{1,0:T(4,128)} reshape(f32[1024]{0:T(1024)} %param.9) | data formatting | bytes 8192 | tf_op jit(solution)/shard_map/reshape | solution.py:370
  1.9 111.4 %shard_map.68 = (f32[1024,128]{1,0:T(8,128)}, f32[3,128]{1,0:T(4,128)}) custom-call(s32[1,128]{1,0:T(1,128)} %bitcast.4, s32[1,128]{1,0:T(1,128)} %bitcast.5, bf16[128,256,256]{2,1,0:T(8,128)(2,1)} %bitcast.3, s32[1024,128]{1,0:T(8,128)} %bits.1, f32[4,256]{1,0:T(4,128)} %reshape.7.shift), custom_call_target="tpu_custom_call" | custom-call | flops 6442450944 | bytes 18874368 | tf_op jit(solution)/shard_map/pallas_call | solution.py:318
  113.3 1.3 %copy.9 = f32[3,128]{1,0:T(4,128)} copy(f32[3,128]{1,0:T(4,128)} %get-tuple-element.8) | data formatting | bytes 3072
  114.6 1.9 %copy.10 = f32[1024,128]{1,0:T(8,128)} copy(f32[1024,128]{1,0:T(8,128)} %get-tuple-element.9) | data formatting | bytes 1048576

commit v7 on v6

--- a/solution.py
+++ b/solution.py
@@ -173,7 +173,7 @@
                         form = form + zg[c, h, d - 1, b].astype(F32) * (scale(a) * total)
                     else:
                         qown[c, h, g, k] = total
-                        form = form + z[c, h, b] * (scale(a) * (total + shift[b:b + 1] * t[par, c, h, b])
+                        form = form + z[c, h, b] * (scale(a) * (total + shift[:, b * BS:(b + 1) * BS] * t[par, c, h, b])
                                                     - t[1 - par, c, h, b])
                 if d:
                     remote(q.at[c, h, g, d - 1], r2.at[c, par, h, g, d - 1], qsend.at[c],
@@ -190,7 +190,7 @@
                 m_w = qown[c, h, g, k]
                 for d in (0, 1, 2):
                     m_w = m_w + r2[c, par, h, g, d, k].astype(F32)
-                new = scale(a) * (m_w + shift[b:b + 1] * t[par, c, h, b]) - t[nxt, c, h, b]
+                new = scale(a) * (m_w + shift[:, b * BS:(b + 1) * BS] * t[par, c, h, b]) - t[nxt, c, h, b]
                 t[nxt, c, h, b] = new
                 land[c, nxt, gy * RB + b, h * HP:(h + 1) * HP] = new.astype(BF16)
 
@@ -367,7 +367,7 @@
         cost_estimate=pl.CostEstimate(
             flops=6 * KT * BS * BS * NP, bytes_accessed=18 * 2**20, transcendentals=0
         ),
-    )(block_rows[0], block_cols[0], blocks[0, 0], probe_bits, shift.reshape(RB, BS))
+    )(block_rows[0], block_cols[0], blocks[0, 0], probe_bits, shift[None])
     return forms, out
 
 

time: 117 us -> 115 us (0.983)
  local copies, waits for them, and re-layouts: 4.41 us -> 3.12 us
    reshape x1 -> x0, local copies, waits for them, and re-layouts: 1.29 us -> none  [body(): shift.reshape(RB, BS)]
where the time goes in v7:
time: 115 us
  Pallas kernels  111 us (97%)
  local copies, waits for them, and re-layouts  3.12 us (3%)
    pallas_call x1, Pallas kernels, body(): pl.pallas_call(kernel, out_shape=(jax.ShapeDtypeStruct((LOC, NP), F32), j...  111 us
    unnamed x2, local copies, waits for them, and re-layouts  3.12 us

profile of v7, /device:TPU:0, one launch (start us, length us, event | category | flops | bytes accessed | tf_op | source)
XLA Modules:
  0.0 115.2 jit_solution(10708240541608263426)
XLA Ops:
  0.6 111.5 %shard_map.68 = (f32[1024,128]{1,0:T(8,128)}, f32[3,128]{1,0:T(4,128)}) custom-call(s32[1,128]{1,0:T(1,128)} %bitcast.6, s32[1,128]{1,0:T(1,128)} %bitcast.7, bf16[128,256,256]{2,1,0:T(8,128)(2,1)} %bitcast.4, s32[1024,128]{1,0:T(8,128)} %bits.1, f32[1,1024]{1,0:T(1,128)} %bitcast.5), custom_call_target="tpu_custom_call" | custom-call | flops 6442450944 | bytes 18874368 | tf_op jit(solution)/shard_map/pallas_call | solution.py:318
  112.1 1.3 %copy.9 = f32[3,128]{1,0:T(4,128)} copy(f32[3,128]{1,0:T(4,128)} %get-tuple-element.8) | data formatting | bytes 3072
  113.4 1.9 %copy.10 = f32[1024,128]{1,0:T(8,128)} copy(f32[1024,128]{1,0:T(8,128)} %get-tuple-element.9) | data formatting | bytes 1048576

commit v8 on v7

--- a/solution.py
+++ b/solution.py
@@ -26,7 +26,7 @@
 
 CHUNKS = ((2, 0), (2, 1), (1, 2), (1, 3), (1, 0), (1, 1),
           (2, 2), (2, 3), (3, 0), (3, 1), (3, 2), (3, 3))
-FIRST = ((0, 4), (6, 4), (4, 2), (10, 2))
+FIRST = ((0, 2), (6, 2), (2, 2), (8, 2), (4, 2), (10, 2))
 
 
 def kernel(rows, cols, blocks_hbm, bits, shift, out_hbm, forms,
@@ -131,14 +131,15 @@
         wait_for(r1.at[c, par, h, g, pl.ds(at, n)], rs1.at[c, par, h, g, m])
 
     def begin(c, par):
+        for pair in ((0, 1), (2, 3)):
+            for g in range(PC):
+                for h in (0, 1):
+                    for m in pair:
+                        fill(c, h, g, m)
+                        send1(c, par, h, g, m)
         for g in range(PC):
             for h in (0, 1):
-                for m in (0, 1):
-                    fill(c, h, g, m)
-                    send1(c, par, h, g, m)
-        for g in range(PC):
-            for h in (0, 1):
-                for m in (2, 3):
+                for m in (4, 5):
                     fill(c, h, g, m)
                 for d in range(4):
                     for k in range(G):
@@ -148,11 +149,11 @@
         for h in (0, 1):
             for m in (0, 1):
                 arrived1(c, par, h, g, m)
-                to, came = FIRST[m + 2][0], FIRST[m][0]
+                to, came = FIRST[m + 4][0], FIRST[m][0]
                 for i in range(2):
                     p[c, h, g, to + i] = (p[c, h, g, to + i].astype(F32)
                                           + r1[c, par, h, g, came + i].astype(F32)).astype(BF16)
-                send1(c, par, h, g, m + 2)
+                send1(c, par, h, g, m + 4)
 
     def scale(a):
         return jnp.where(a == 0, 1.0, 2.0).astype(F32)
@@ -160,7 +161,7 @@
     def second(c, a, par, g):
         for h in (0, 1):
             form = jnp.zeros((HP, BS), F32)
-            for m in (2, 3):
+            for m in (2, 3, 4, 5):
                 arrived1(c, par, h, g, m)
             for d in (2, 1, 3, 0):
                 up, down = (4 + d, 8 + d) if d < 2 else (d, 8 + d)
@@ -356,7 +357,7 @@
             dma((KT // LOAD,)), dma, dma,
             dma((NC,)), dma((NC,)),
             dma, dma,
-            dma((NC, 2, 2, PC, 4)),
+            dma((NC, 2, 2, PC, 6)),
             dma((NC, 2, 2, PC, 3)),
             dma((NC, 2, 3)), dma((NC, 2, 3)),
             dma((3, 3)), dma((3, 3)),

time: 115 us -> 113 us (0.983)
  Pallas kernels: 111 us -> 109 us
    pallas_call x1, Pallas kernels: 111 us -> 109 us  [body(): pl.pallas_call(kernel, out_shape=(jax.ShapeDtypeStruct((LOC, NP), F32), j...]
where the time goes in v8:
time: 113 us
  Pallas kernels  109 us (96%)
  local copies, waits for them, and re-layouts  3.12 us (3%)
    pallas_call x1, Pallas kernels, body(): pl.pallas_call(kernel, out_shape=(jax.ShapeDtypeStruct((LOC, NP), F32), j...  109 us
    unnamed x2, local copies, waits for them, and re-layouts  3.12 us

profile of v8, /device:TPU:0, one launch (start us, length us, event | category | flops | bytes accessed | tf_op | source)
XLA Modules:
  0.0 112.9 jit_solution(3184328500440816835)
XLA Ops:
  0.6 109.1 %shard_map.68 = (f32[1024,128]{1,0:T(8,128)}, f32[3,128]{1,0:T(4,128)}) custom-call(s32[1,128]{1,0:T(1,128)} %bitcast.6, s32[1,128]{1,0:T(1,128)} %bitcast.7, bf16[128,256,256]{2,1,0:T(8,128)(2,1)} %bitcast.4, s32[1024,128]{1,0:T(8,128)} %bits.1, f32[1,1024]{1,0:T(1,128)} %bitcast.5), custom_call_target="tpu_custom_call" | custom-call | flops 6442450944 | bytes 18874368 | tf_op jit(solution)/shard_map/pallas_call | solution.py:319
  109.8 1.3 %copy.9 = f32[3,128]{1,0:T(4,128)} copy(f32[3,128]{1,0:T(4,128)} %get-tuple-element.8) | data formatting | bytes 3072
  111.0 1.9 %copy.10 = f32[1024,128]{1,0:T(8,128)} copy(f32[1024,128]{1,0:T(8,128)} %get-tuple-element.9) | data formatting | bytes 1048576

commit v9 on v8

--- a/solution.py
+++ b/solution.py
@@ -20,6 +20,7 @@
 F32 = jnp.float32
 BF16 = jnp.bfloat16
 UNROLL = 32
+LATER = 2
 LOAD = 16
 ORDER = ('w.0', 'm0.0', 's0.1', 'm1.0', 's1.1', 'm2.0', 's2.1', 'm3.0', 's3.1', 'b.0', 'f0.1', 'f1.1', 'f2.1', 'f3.1', 'e.1', 'h0.0', 'h1.0', 'h2.0', 'h3.0')
 
@@ -136,7 +137,8 @@
                 for h in (0, 1):
                     for m in pair:
                         fill(c, h, g, m)
-                        send1(c, par, h, g, m)
+                        if m < 2 or g < PC - LATER:
+                            send1(c, par, h, g, m)
         for g in range(PC):
             for h in (0, 1):
                 for m in (4, 5):
@@ -154,6 +156,8 @@
                     p[c, h, g, to + i] = (p[c, h, g, to + i].astype(F32)
                                           + r1[c, par, h, g, came + i].astype(F32)).astype(BF16)
                 send1(c, par, h, g, m + 4)
+                if g < LATER:
+                    send1(c, par, h, g + PC - LATER, m + 2)
 
     def scale(a):
         return jnp.where(a == 0, 1.0, 2.0).astype(F32)

time: 113 us -> 112 us (level)
  no operation moved by 1% of the time
where the time goes in v9:
time: 112 us
  Pallas kernels  108 us (96%)
  local copies, waits for them, and re-layouts  3.12 us (3%)
    pallas_call x1, Pallas kernels, body(): pl.pallas_call(kernel, out_shape=(jax.ShapeDtypeStruct((LOC, NP), F32), j...  108 us
    unnamed x2, local copies, waits for them, and re-layouts  3.12 us

profile of v9, /device:TPU:0, one launch (start us, length us, event | category | flops | bytes accessed | tf_op | source)
XLA Modules:
  0.0 111.9 jit_solution(9281598437666674874)
XLA Ops:
  0.6 108.2 %shard_map.68 = (f32[1024,128]{1,0:T(8,128)}, f32[3,128]{1,0:T(4,128)}) custom-call(s32[1,128]{1,0:T(1,128)} %bitcast.6, s32[1,128]{1,0:T(1,128)} %bitcast.7, bf16[128,256,256]{2,1,0:T(8,128)(2,1)} %bitcast.4, s32[1024,128]{1,0:T(8,128)} %bits.1, f32[1,1024]{1,0:T(1,128)} %bitcast.5), custom_call_target="tpu_custom_call" | custom-call | flops 6442450944 | bytes 18874368 | tf_op jit(solution)/shard_map/pallas_call | solution.py:323
  108.8 1.3 %copy.9 = f32[3,128]{1,0:T(4,128)} copy(f32[3,128]{1,0:T(4,128)} %get-tuple-element.8) | data formatting | bytes 3072
  110.1 1.9 %copy.10 = f32[1024,128]{1,0:T(8,128)} copy(f32[1024,128]{1,0:T(8,128)} %get-tuple-element.9) | data formatting | bytes 1048576
